TPU v7x, 256 devices: a whole 4x4x8 slice. The times are simulated.
256 devices in a mesh: group: 32 (over z_hi, x, core), bulk: 8 (over y, z_lo).
Axes of the slice: x: 4, y: 4, z: 8 (z_hi: 4, z_lo: 2; z = z_hi * 2 + z_lo), core: 2. Of those that a mesh axis runs over, the one named last changes fastest.
Arguments:
- picture_feature_vectors: bfloat16 [32, 8, 384, 1152], P('group', 'bulk'), may hold values from -0.1875 to 0.1875
- caption_feature_vectors: bfloat16 [32, 8, 384, 1152], P('group', 'bulk'), may hold values from -0.1875 to 0.1875
- sharpness_factor: float32 [], replicated, may hold values from 4 to 8
- score_offset: float32 [], replicated, may hold values from -4 to -2
- difficult_decoy_tile_numbers: int32 [32, 8, 8, 2], P('group', 'bulk'), may hold values from -1 to 2, as said below
Outputs:
- image_grad: float32 [32, 8, 384, 1152], P('group', 'bulk')
- text_grad: float32 [32, 8, 384, 1152], P('group', 'bulk')
Inputs may be any that keep to these rules, and one draw needn't show every extreme that they name: `difficult_decoy_tile_numbers`: toward each bulk index o, the first slots of a device hold block numbers n (rows n * 128 to n * 128 + 127 of the texts of the device with the same group index and bulk index o) and the remaining slots are -1; all slots toward a device's own bulk index are -1; in group index 0 every device with bulk index other than 0 fills all 2 slots toward bulk index 0.
All inputs are finite; a program needn't handle non-finite values.
Results may differ from a plain program's by a relative error of at most 0.0045.
Values may be sent and summed in bfloat16 or wider, within the bound.
No kernel may reach another device: no remote copies, remote signals or barrier semaphores. Data moves between devices by JAX's collectives and lax.ppermute only.
A program may use at most 128 MiB of HBM per device.

v0:
```python
import jax
import jax.numpy as jnp
from jax import lax
from jax.experimental import pallas as pl
from jax.experimental.pallas import tpu as pltpu
from jax.sharding import Mesh, PartitionSpec as P

ROWS = 384
HALF = 192
BLOCK = 128
WIDTH = 1152
GROUP = ("zh", "x", "c")
BULK = ("y", "zl")
BF16 = jnp.bfloat16
F32 = jnp.float32
SM = pl.BlockSpec(memory_space=pltpu.SMEM)
ANY = pl.BlockSpec(memory_space=pltpu.HBM)
FREE = pl.BlockSpec(memory_space=pl.ANY)
WHOLE, WHOLE32 = ((ROWS, WIDTH), BF16), ((ROWS, WIDTH), F32)


def vm(rows, width=WIDTH, dtype=BF16):
    return pltpu.VMEM((rows, width), dtype)


def ring(x, axis, by):
    size = lax.axis_size(axis)
    return lax.ppermute(x, axis, [(i, (i + by) % size) for i in range(size)])


def call(body, outs, args, scratch, name, smem=0, space=ANY, limit=60, flops=8_000_000_000):
    def kernel(*refs):
        body(Copies(refs[-1]), *refs[:-1])

    return pl.pallas_call(
        kernel,
        out_shape=[jax.ShapeDtypeStruct(s, d) for s, d in outs],
        in_specs=[SM] * smem + [space] * (len(args) - smem),
        out_specs=[ANY] * len(outs),
        scratch_shapes=list(scratch) + [pltpu.SemaphoreType.DMA((32,))],
        cost_estimate=pl.CostEstimate(flops=flops, bytes_accessed=0, transcendentals=0),
        compiler_params=pltpu.CompilerParams(vmem_limit_bytes=limit * 2**20),
        name=name,
    )(*args)


class Copies:
    def __init__(self, sems):
        self.sems, self.count = sems, 0

    def go(self, src, dst):
        copy = self.of(src, dst)
        copy.start()
        return copy

    def of(self, src, dst):
        copy = pltpu.make_async_copy(src, dst, self.sems.at[self.count])
        self.count += 1
        return copy

    def pick(self, when, src, other, dst):
        copy = self.of(src, dst)
        instead = pltpu.make_async_copy(other, dst, self.sems.at[self.count - 1])
        pl.when(when)(copy.start)
        pl.when(jnp.logical_not(when))(instead.start)
        return copy


def nt(a, b):
    return lax.dot_general(a, b, (((1,), (1,)), ((), ())), preferred_element_type=F32)


def nn(a, b):
    return lax.dot_general(a, b, (((1,), (0,)), ((), ())), preferred_element_type=F32)


def tn(a, b):
    return lax.dot_general(a, b, (((0,), (0,)), ((), ())), preferred_element_type=F32)


def inverse_length(values):
    return lax.rsqrt(jnp.sum(values * values, axis=-1, keepdims=True) + 1e-06)


def unit_kernel(
    copies, ids_ref, cap_ref, pic_ref, text_out, image_out, wrap_out, even_out, low_out,
    cap, pic, text, image, wrap, even, low,
):
    x = lax.axis_index("x")
    come = [
        [copies.go(src.at[pl.ds(k * HALF, HALF)], dst.at[pl.ds(k * HALF, HALF)])
         for src, dst in ((cap_ref, cap), (pic_ref, pic))]
        for k in range(2)
    ]
    row = lax.broadcasted_iota(jnp.int32, (16, BLOCK), 0)
    image[pl.ds(ROWS, 16), :] = jnp.zeros((16, WIDTH), BF16)
    for n in range(3):
        count = jnp.zeros((16, BLOCK), F32)
        for owner in range(8):
            hit = [jnp.where(ids_ref[c, owner] == n, 1.0, 0.0) for c in range(2)]
            count = jnp.where(row == owner, hit[0] + hit[1], count)
        image[pl.ds(ROWS, 16), pl.ds(n * BLOCK, BLOCK)] = count.astype(BF16)
    leave = []
    for k in range(2):
        at = pl.ds(k * HALF, HALF)
        come[k][0].wait()
        v = cap[at, :].astype(F32)
        t = (v * inverse_length(v)).astype(BF16)
        text[at, :] = t
        come[k][1].wait()
        v = pic[at, :].astype(F32)
        i = (v * inverse_length(v)).astype(BF16)
        image[at, :] = i
        wrap[at, :] = jnp.where(x >= 2, t, i)
        even[at, :] = jnp.where(lax.rem(x, 2) == 0, t, i)
        low[at, :] = jnp.where(x < 2, t, i)
        for src, dst in ((text, text_out), (wrap, wrap_out), (even, even_out), (low, low_out)):
            leave.append(copies.go(src.at[at], dst.at[at]))
        if k == 0:
            leave.append(copies.go(image.at[at], image_out.at[at]))
        else:
            rest = pl.ds(HALF, HALF + 16)
            leave.append(copies.go(image.at[rest], image_out.at[rest]))
    for copy in leave:
        copy.wait()


def weights(scores, par_ref):
    half = par_ref[0] * 0.5
    return half + half * jnp.tanh(half * scores + par_ref[1] * 0.5)


def slot_count(counts, owner, block):
    values = counts[pl.ds(0, 16), pl.ds(block * BLOCK, BLOCK)].astype(F32)
    row = lax.broadcasted_iota(jnp.int32, (16, BLOCK), 0)
    return jnp.sum(jnp.where(row == owner, values, 0.0), axis=0, keepdims=True)


def hard_weights(text, x_scr, wt_ref, row, par_ref, near, far, owner, own):
    for j in range(3):
        w = weights(nt(text, x_scr[pl.ds(j * 256, 256), :]), par_ref)
        if own and j < 2:
            r = lax.broadcasted_iota(jnp.int32, (ROWS, 256), 0)
            q = lax.broadcasted_iota(jnp.int32, (ROWS, 256), 1) + j * 256
            w = jnp.where(r == q, w - par_ref[0], w)
        w = w.astype(BF16)
        for n in range(3):
            rows = slice(n * BLOCK, (n + 1) * BLOCK)
            for h in range(2):
                col = j * 256 + h * 128
                part = w[rows, h * 128 : (h + 1) * 128]
                if col >= ROWS or not own:
                    count = slot_count(near if col < ROWS else far, owner, n)
                    part = (part.astype(F32) * count).astype(BF16)
                wt_ref[pl.ds(row + n * BLOCK, BLOCK), pl.ds(col, 128)] = part


def owners():
    y, zl, core = lax.axis_index("y"), lax.axis_index("zl"), lax.axis_index("c")
    return [lax.rem(y + step, 4) * 2 + zl for step in (3 - 2 * core, 1 + 2 * core, 0, 2)]


def fetch_images(copies, image_ref, other_ref, x_scr, near, far):
    rows, rest = pl.ds(0, ROWS), pl.ds(ROWS, 16)
    return [
        copies.go(image_ref.at[rest], near),
        copies.go(other_ref.at[rest], far),
        copies.go(image_ref.at[rows], x_scr.at[rows]),
        copies.go(other_ref.at[rows], x_scr.at[pl.ds(ROWS, ROWS)]),
    ]


def hard_kernel(
    copies, par_ref, image_ref, other_ref, one_ref, two_ref, text_ref, after_ref,
    early_out, late_out, gt_out, wt_out, x_scr, near, far, t_scr, early, late, gt, wt,
):
    images = fetch_images(copies, image_ref, other_ref, x_scr, near, far)
    texts = [copies.go(ref, t_scr.at[k]) for k, ref in enumerate((one_ref, two_ref, text_ref))]
    owner = owners()
    for copy in images:
        copy.wait()
    leave = []
    for k in range(3):
        texts[k].wait()
        hard_weights(t_scr[k], x_scr, wt, k * ROWS, par_ref, near, far, owner[k], k == 2)
        p = nn(wt[pl.ds(k * ROWS, ROWS), :], x_scr[...])
        if k == 0:
            early[...] = p.astype(BF16)
        else:
            (late, gt)[k - 1][...] = p
        src, dst = ((early, early_out), (late, late_out), (gt, gt_out))[k]
        leave.append(copies.go(src, dst))
    leave.append(copies.go(wt, wt_out))
    for copy in leave:
        copy.wait()


def opposite_kernel(
    copies, par_ref, image_ref, other_ref, opp_ref, after_ref, then_ref, return_out, wt_out,
    x_scr, near, far, text, back, wt,
):
    images = fetch_images(copies, image_ref, other_ref, x_scr, near, far)
    images.append(copies.go(opp_ref, text))
    for copy in images:
        copy.wait()
    hard_weights(text[...], x_scr, wt, 0, par_ref, near, far, owners()[3], False)
    leave = [copies.go(wt, wt_out)]
    back[...] = nn(wt[...], x_scr[...]).astype(BF16)
    leave.append(copies.go(back, return_out))
    for copy in leave:
        copy.wait()


def image_kernel(
    copies, wt3_ref, wt_ref, one_ref, two_ref, text_ref, opp_ref, image_ref, from_one,
    from_two, from_three, aw, bw, far_out, near_out, own_out, w_scr, t_scr, far, near,
):
    come = [
        copies.go(wt3_ref, w_scr.at[pl.ds(0, 3 * ROWS)]),
        copies.go(wt_ref, w_scr.at[pl.ds(3 * ROWS, ROWS)]),
    ]
    for k, ref in enumerate((one_ref, two_ref, text_ref, opp_ref)):
        come.append(copies.go(ref, t_scr.at[pl.ds(k * ROWS, ROWS)]))
    image = image_ref.at[pl.ds(0, ROWS)]
    leave = [copies.pick(lax.axis_index("c") == 0, text_ref, image, own_out.at[0])]
    x = lax.axis_index("x")
    inner = jnp.logical_or(x == 1, x == 2)
    for k, ref in enumerate((from_one, from_two)):
        leave.append(copies.go(ref, own_out.at[k + 1]))
    leave.append(copies.pick(inner, from_three, aw, own_out.at[3]))
    leave.append(copies.go(bw, own_out.at[4]))
    for copy in come:
        copy.wait()
    far[...] = tn(w_scr[:, ROWS:], t_scr[...]).astype(BF16)
    leave.append(copies.go(far, far_out))
    near[...] = tn(w_scr[:, :ROWS], t_scr[...])
    leave.append(copies.go(near, near_out))
    for copy in leave:
        copy.wait()


def attend(mine, scr, w_scr, par_ref, count):
    for j in range(count * 3 // 2):
        at = pl.ds(j * 256, 256)
        w_scr[:, at] = weights(nt(mine, scr[at, :]), par_ref).astype(BF16)
    return nn(w_scr[:, : count * ROWS], scr[: count * ROWS, :])


def cycle_kernel(
    copies, par_ref, image_ref, text_ref, own, sib, gi_ref, gt_ref,
    after_ref, early_ref, gi_out, gt_out, image, text, gi, gt, t_scr, i_scr, w_scr,
):
    x, core = lax.axis_index("x"), lax.axis_index("c")
    come = []
    for low, mine_ref, mine, grad_ref, grad, scr in (
        (True, image_ref, image, gi_ref, gi, t_scr),
        (False, text_ref, text, gt_ref, gt, i_scr),
    ):
        d = x if low else 3 - x
        e = core if low else 1 - core
        slot = lambda k: scr.at[pl.ds(k * ROWS, ROWS)]

        def place(i, beyond):
            inside = jnp.bitwise_xor(x, jnp.clip(i if low else 3 - i, 0, 3))
            return jnp.where(i >= 0, inside, beyond)

        swapped = jnp.logical_and(d == 0, e == 1)
        here = [
            copies.go(mine_ref.at[pl.ds(0, ROWS)], mine),
            copies.go(own.at[place(d - 1, 3)], slot(0)),
            copies.go(own.at[place(d - 2, 4)], slot(1)),
            copies.go(sib.at[place(d - 1 + e, 3)], slot(2)),
            copies.go(sib.at[place(d - 2 + e, jnp.where(swapped, 3, 4))], slot(3)),
        ]
        here.append(copies.go(grad_ref, grad))
        come.append(here)
    leave = []
    for here, mine, grad, scr, out in (
        (come[0], image, gi, t_scr, gi_out),
        (come[1], text, gt, i_scr, gt_out),
    ):
        for copy in here:
            copy.wait()
        grad[...] += attend(mine[...], scr, w_scr, par_ref, 4)
        leave.append(copies.go(grad, out))
    for copy in leave:
        copy.wait()


def add_kernel(copies, late_ref, return_ref, after_ref, then_ref, out_ref, late, back, out):
    come = [copies.go(late_ref, late), copies.go(return_ref, back)]
    for copy in come:
        copy.wait()
    out[...] = (late[...] + back[...].astype(F32)).astype(BF16)
    copies.go(out, out_ref).wait()


def gate_kernel(block_ref, after_ref, out_ref):
    pass


def through_norm(raw, grads):
    values = raw.astype(F32)
    inv = inverse_length(values)
    unit = values * inv
    inner = jnp.sum(unit * grads, axis=-1, keepdims=True)
    return (grads - unit * inner) * inv


def last_kernel(
    copies, par_ref, f, f1, image_ref, text_ref, pic_ref, gi_ref, back_ref, cap_ref, gt_ref,
    early_ref, late_ref, image_out, text_out,
    scr, w_scr, mine, more, pic, gi, back, cap, gt, early, late,
):
    x = lax.axis_index("x")
    come = [
        copies.go(f, scr.at[pl.ds(0, ROWS)]),
        copies.go(f1, scr.at[pl.ds(ROWS, ROWS)]),
        copies.pick(x <= 1, image_ref.at[pl.ds(0, ROWS)], text_ref, mine),
    ]
    rest = [
        copies.go(src, dst)
        for src, dst in (
            (pic_ref, pic), (gi_ref, gi), (back_ref, back), (cap_ref, cap), (gt_ref, gt),
            (early_ref, early), (late_ref, late),
        )
    ]
    for copy in come:
        copy.wait()

    @pl.when(jnp.logical_or(x == 1, x == 2))
    def _():
        more[...] = attend(mine[...], scr, w_scr, par_ref, 2)

    for copy in rest:
        copy.wait()
    leave = []
    for k in range(3):
        at = pl.ds(k * BLOCK, BLOCK)
        g = gi[at, :] + back[at, :].astype(F32)
        g = jnp.where(x == 1, g + more[at, :], g)
        gi[at, :] = through_norm(pic[at, :], g)
        leave.append(copies.go(gi.at[at], image_out.at[at]))
        g = gt[at, :] + early[at, :].astype(F32) + late[at, :].astype(F32)
        g = jnp.where(x == 2, g + more[at, :], g)
        gt[at, :] = through_norm(cap[at, :], g)
        leave.append(copies.go(gt.at[at], text_out.at[at]))
    for copy in leave:
        copy.wait()


def gate(block, after):
    return pl.pallas_call(
        gate_kernel,
        out_shape=jax.ShapeDtypeStruct(block.shape, block.dtype),
        in_specs=[FREE, FREE],
        out_specs=FREE,
        input_output_aliases={0: 0},
        compiler_params=pltpu.CompilerParams(vmem_limit_bytes=2**20),
        name="gate",
    )(block, after)


def local(pictures, captions, sharpness, offset, tile_numbers):
    pics, caps = pictures[0, 0], captions[0, 0]
    par = jnp.stack([sharpness, offset])
    counts = [vm(16), vm(16)]
    text, image, wrap, even, low = call(
        unit_kernel,
        [WHOLE, ((ROWS + 16, WIDTH), BF16), WHOLE, WHOLE, WHOLE],
        (tile_numbers[0, 0].T, caps, pics),
        [vm(ROWS), vm(ROWS), vm(ROWS), vm(ROWS + 16), vm(ROWS), vm(ROWS), vm(ROWS)],
        "unit",
        1,
    )

    def along_y(block, way):
        pairs = []
        for y in range(4):
            pairs += [(y, (y + way) % 4), (4 + y, 4 + (y - way) % 4)]
        return lax.ppermute(block, ("c", "y"), pairs)

    turn = lambda x, c: x * 2 + c
    with jax.named_scope("one"):
        text_one = along_y(text, 1)
    with jax.named_scope("other"):
        other = ring(image, "zl", 1)
    with jax.named_scope("two"):
        text_two = along_y(text, -1)
    with jax.named_scope("hop"):
        hop = lax.ppermute(
            wrap,
            ("x", "c"),
            [(turn(x, 0), turn(x, 0)) for x in range(4)]
            + [(turn(a, 1), turn(b, 1)) for a, b in ((3, 0), (2, 1), (1, 2), (0, 3))],
        )
    with jax.named_scope("near"):
        from_one = lax.ppermute(even, "x", [(0, 1), (1, 0), (2, 3), (3, 2)])
    with jax.named_scope("mid"):
        from_three = lax.ppermute(low, "x", [(1, 2), (2, 1)])
    with jax.named_scope("far"):
        from_two = lax.ppermute(gate(low, from_one), "x", [(0, 2), (2, 0), (1, 3), (3, 1)])
    with jax.named_scope("opp"):
        text_opp = along_y(text_one, 1)
    hop = gate(hop, other)

    def over(pairs):
        sends = []
        for z in range(4):
            for a, b, c, d in pairs:
                sends.append((z * 8 + turn(a, c), (z + d) % 4 * 8 + turn(b, c)))
        return lax.ppermute(hop, GROUP, sends)

    with jax.named_scope("over_a"):
        over_a = over([(3, 0, 0, 1), (0, 3, 0, -1), (0, 0, 1, 1), (3, 3, 1, -1)])
    with jax.named_scope("over_b"):
        over_b = over([(2, 0, 0, 1), (1, 3, 0, -1), (1, 0, 1, 1), (2, 3, 1, -1)])

    part_early, part_late, grad_text, wt3 = call(
        hard_kernel,
        [WHOLE, WHOLE32, WHOLE32, ((3 * ROWS, 2 * ROWS), BF16)],
        (par, image, other, text_one, text_two, text, hop),
        [vm(2 * ROWS), *counts, pltpu.VMEM((3, ROWS, WIDTH), BF16), vm(ROWS),
         vm(ROWS, dtype=F32), vm(ROWS, dtype=F32), vm(3 * ROWS, 2 * ROWS)],
        "hard",
        1,
    )
    with jax.named_scope("early"):
        early = along_y(part_early, -1)
    part_opp, wt = call(
        opposite_kernel,
        [WHOLE, ((ROWS, 2 * ROWS), BF16)],
        (par, image, other, text_opp, part_early, from_three),
        [vm(2 * ROWS), *counts, vm(ROWS), vm(ROWS), vm(ROWS, 2 * ROWS)],
        "opposite",
        1,
    )
    with jax.named_scope("carried"):
        carried = along_y(part_opp, 1)
    grad_far, grad_image, own = call(
        image_kernel,
        [WHOLE, WHOLE32, ((5, ROWS, WIDTH), BF16)],
        (wt3, wt, text_one, text_two, text, text_opp, image, from_one, from_two, from_three,
         over_a, over_b),
        [vm(4 * ROWS, 2 * ROWS), vm(4 * ROWS), vm(ROWS), vm(ROWS, dtype=F32)],
        "image_side",
    )
    with jax.named_scope("back"):
        grad_back = ring(grad_far, "zl", 1)
    part_late = call(
        add_kernel,
        [WHOLE],
        (part_late, carried, grad_far, early),
        [vm(ROWS, dtype=F32), vm(ROWS), vm(ROWS)],
        "add",
        flops=1,
    )[0]
    with jax.named_scope("late"):
        late = along_y(part_late, 1)

    with jax.named_scope("sib"):
        sib = ring(gate(own, part_late), "c", 1)

    with jax.named_scope("over_f"):
        over_f = lax.ppermute(over_a, "x", [(0, 1), (3, 2)])
    grad_image, grad_text = call(
        cycle_kernel,
        [WHOLE32, WHOLE32],
        (par, image, text, own, sib, grad_image, grad_text, part_late, early),
        [vm(ROWS), vm(ROWS), vm(ROWS, dtype=F32), vm(ROWS, dtype=F32), vm(4 * ROWS),
         vm(4 * ROWS), vm(ROWS, 4 * ROWS)],
        "cycle",
        1,
        flops=1,
    )
    over_f = gate(over_f, grad_image)
    with jax.named_scope("over_f1"):
        over_f1 = lax.ppermute(
            over_f, ("x", "c"), [(turn(1, 1), turn(1, 0)), (turn(2, 0), turn(2, 1))]
        )
    image_grad, text_grad = call(
        last_kernel,
        [WHOLE32, WHOLE32],
        (par, over_f, over_f1, image, text, pics, grad_image, grad_back, caps, grad_text,
         early, late),
        [vm(2 * ROWS), vm(ROWS, 2 * ROWS), vm(ROWS), vm(ROWS, dtype=F32), vm(ROWS),
         vm(ROWS, dtype=F32), vm(ROWS), vm(ROWS), vm(ROWS, dtype=F32), vm(ROWS), vm(ROWS)],
        "last",
        1,
        FREE,
        24,
    )
    return (image_grad[None, None], text_grad[None, None])


def solution(mesh):
    fine = Mesh(mesh.devices.reshape(4, 4, 2, 4, 2), GROUP + BULK)
    spec = P(GROUP, BULK, None, None)
    return jax.shard_map(
        local,
        mesh=fine,
        in_specs=(spec, spec, P(), P(), spec),
        out_specs=(spec, spec),
        check_vma=False,
    )
```

profile of v0, /device:TPU:3, one launch (start us, length us, event | category | flops | bytes accessed | tf_op | source)
XLA Modules:
  0.0 276.3 jit_solution(18382386438062679120)
XLA Ops:
  0.6 4.4 %unit.1 = (bf16[384,1152]{1,0:T(8,128)(2,1)}, bf16[400,1152]{1,0:T(8,128)(2,1)}, bf16[384,1152]{1,0:T(8,128)(2,1)}, bf16[384,1152]{1,0:T(8,128)(2,1)}, bf16[384,1152]{1,0:T(8,128)(2,1)}) custom-call(s32[2,8]{1,0:T(2,128)} %bitcast.15, bf16[384,1152]{1,0:T(8,128)(2,1)} %bitcast.11, bf16[384,1152]{1,0:T(8,128)(2,1)} %bitcast.13), custom_call_target="tpu_custom_call" | custom-call | flops 8000000000 | tf_op jit(solution)/shard_map/unit/pallas_call | solution.py:35
  5.0 2.8 %collective-permute-start.4 = (bf16[384,1152]{1,0:T(8,128)(2,1)}, bf16[384,1152]{1,0:T(8,128)(2,1)}, u32[]{:S(2)}, u32[]{:S(2)}) collective-permute-start(bf16[384,1152]{1,0:T(8,128)(2,1)} %get-tuple-element.22.refs_5_.refs_4_.refs_2_), channel_id=1, source_target_pairs={{0,2},{8,14},{2,4},{10,8},{4,6},{12,10},{6,0},{14,12},{1,3},{9,15}... | collective-permute-start | bytes 2654216 | tf_op jit(solution)/shard_map/one/ppermute | solution.py:381
  7.8 3.1 %collective-permute-start.7 = (bf16[384,1152]{1,0:T(8,128)(2,1)}, bf16[384,1152]{1,0:T(8,128)(2,1)}, u32[]{:S(2)}, u32[]{:S(2)}) collective-permute-start(bf16[384,1152]{1,0:T(8,128)(2,1)} %get-tuple-element.25.block_ref), channel_id=1, source_target_pairs={{16,32},{32,16},{17,33},{33,17},{18,34},{34,18},{19,35},{35,19},{2... | collective-permute-start | bytes 2654216 | tf_op jit(solution)/shard_map/mid/ppermute | solution.py:400
  10.9 1.7 collective-permute-start.1
  12.7 2.5 collective-permute-start
  15.1 3.0 %collective-permute-done.4.refs_3_.refs_2_ = bf16[384,1152]{1,0:T(8,128)(2,1)} collective-permute-done((bf16[384,1152]{1,0:T(8,128)(2,1)}, bf16[384,1152]{1,0:T(8,128)(2,1)}, u32[]{:S(2)}, u32[]{:S(2)}) %collective-permute-start.4) | collective-permute-done | bytes 884768 | tf_op jit(solution)/shard_map/one/ppermute | solution.py:381
  18.9 12.8 %collective-permute-done.7.refs_5_.refs_9_ = bf16[384,1152]{1,0:T(8,128)(2,1)} collective-permute-done((bf16[384,1152]{1,0:T(8,128)(2,1)}, bf16[384,1152]{1,0:T(8,128)(2,1)}, u32[]{:S(2)}, u32[]{:S(2)}) %collective-permute-start.7) | collective-permute-done | bytes 884768 | tf_op jit(solution)/shard_map/mid/ppermute | solution.py:400
  36.8 23.0 %collective-permute-done.block_ref = bf16[384,1152]{1,0:T(8,128)(2,1)S(1)} collective-permute-done((bf16[384,1152]{1,0:T(8,128)(2,1)}, bf16[384,1152]{1,0:T(8,128)(2,1)S(1)}, u32[]{:S(2)}, u32[]{:S(2)}) %collective-permute-start) | collective-permute-done | bytes 884768 | tf_op jit(solution)/shard_map/hop/ppermute | solution.py:391
  62.8 10.6 %hard.1 = (bf16[384,1152]{1,0:T(8,128)(2,1)}, f32[384,1152]{1,0:T(8,128)}, f32[384,1152]{1,0:T(8,128)}, bf16[1152,768]{1,0:T(8,128)(2,1)}) custom-call(f32[2]{0:T(128)} %pad_maximum_fusion.refs_0_, bf16[400,1152]{1,0:T(8,128)(2,1)} %get-tuple-element.21.refs_1_.refs_6_.refs_3_, bf16[400,1152]{1,0:T(8,128)(2,1)} %copy-done.7, ...), custom_call_target="tpu_custom_call" | custom-call | flops 8000000000 | tf_op jit(solution)/shard_map/hard/pallas_call | solution.py:35
  73.7 5.5 %opposite.1 = (bf16[384,1152]{1,0:T(8,128)(2,1)}, bf16[384,768]{1,0:T(8,128)(2,1)}) custom-call(f32[2]{0:T(128)} %pad_maximum_fusion.refs_0_, bf16[400,1152]{1,0:T(8,128)(2,1)} %get-tuple-element.21.refs_1_.refs_6_.refs_3_, bf16[400,1152]{1,0:T(8,128)(2,1)} %copy-done.7, bf16[384,1152]{1,0:T(8,128)(2,1)} %collective-permute-done.6.refs_3_.refs_5_, ...), custom_call_target="tpu_custom_call" | custom-call | flops 8000000000 | tf_op jit(solution)/shard_map/opposite/pallas_call | solution.py:35
  79.2 2.7 collective-permute-start.11
  82.8 135.4 %image_side.1 = (bf16[384,1152]{1,0:T(8,128)(2,1)}, f32[384,1152]{1,0:T(8,128)}, bf16[5,384,1152]{2,1,0:T(8,128)(2,1)}) custom-call(bf16[1152,768]{1,0:T(8,128)(2,1)} %get-tuple-element.23.refs_0_, bf16[384,768]{1,0:T(8,128)(2,1)} %get-tuple-element.26.refs_1_, bf16[384,1152]{1,0:T(8,128)(2,1)} %collective-permute-done.4.refs_3_.refs_2_, ...), custom_call_target="tpu_custom_call" | custom-call | flops 8000000000 | tf_op jit(solution)/shard_map/image_side/pallas_call | solution.py:35
  218.3 4.7 %copy.13.block_ref = bf16[5,384,1152]{2,1,0:T(8,128)(2,1)} copy(bf16[5,384,1152]{2,1,0:T(8,128)(2,1)} %get-tuple-element.28.refs_3_) | data formatting | bytes 8847360
  224.2 3.0 %add.1.after_ref.refs_7_ = bf16[384,1152]{1,0:T(8,128)(2,1)} custom-call(f32[384,1152]{1,0:T(8,128)} %get-tuple-element.29.refs_0_, bf16[384,1152]{1,0:T(8,128)(2,1)} %copy-done.18, bf16[384,1152]{1,0:T(8,128)(2,1)} %get-tuple-element.31.refs_2_, bf16[384,1152]{1,0:T(8,128)(2,1)} %copy-done.2), custom_call_target="tpu_custom_call" | custom-call | flops 1 | tf_op jit(solution)/shard_map/add/pallas_call | solution.py:35
  227.2 2.2 copy-done
  229.5 2.1 copy-done.1
  231.5 2.5 collective-permute-start.13
  235.5 5.8 %collective-permute-done.13.refs_4_ = bf16[5,384,1152]{2,1,0:T(8,128)(2,1)S(1)} collective-permute-done((bf16[5,384,1152]{2,1,0:T(8,128)(2,1)}, bf16[5,384,1152]{2,1,0:T(8,128)(2,1)S(1)}, u32[]{:S(2)}, u32[]{:S(2)}) %collective-permute-start.13) | collective-permute-done | bytes 4423712 | tf_op jit(solution)/shard_map/sib/ppermute | solution.py:28
  241.4 2.1 copy-done.17
  243.4 11.7 %cycle.1 = (f32[384,1152]{1,0:T(8,128)}, f32[384,1152]{1,0:T(8,128)}) custom-call(f32[2]{0:T(128)} %pad_maximum_fusion.refs_0_, bf16[400,1152]{1,0:T(8,128)(2,1)} %get-tuple-element.21.refs_1_.refs_6_.refs_3_, bf16[384,1152]{1,0:T(8,128)(2,1)} %get-tuple-element.22.refs_5_.refs_4_.refs_2_, bf16[5,384,1152]{2,1,0:T(8,128)(2,1)} %get-tuple-element.28.refs_3_, ...), custom_call_target="tpu_custom_call" | custom-call | flops 1 | tf_op jit(solution)/shard_map/cycle/pallas_call | solution.py:35
  255.2 5.2 %collective-permute-done.3.block_ref = bf16[384,1152]{1,0:T(8,128)(2,1)S(1)} collective-permute-done((bf16[384,1152]{1,0:T(8,128)(2,1)}, bf16[384,1152]{1,0:T(8,128)(2,1)S(1)}, u32[]{:S(2)}, u32[]{:S(2)}) %collective-permute-start.3) | collective-permute-done | bytes 884768 | tf_op jit(solution)/shard_map/over_f/ppermute | solution.py:465
  261.9 3.5 %collective-permute-start.14 = (bf16[384,1152]{1,0:T(8,128)(2,1)S(1)}, bf16[384,1152]{1,0:T(8,128)(2,1)S(1)}, u32[]{:S(2)}, u32[]{:S(2)}) collective-permute-start(bf16[384,1152]{1,0:T(8,128)(2,1)S(1)} %gate.7.refs_1_), channel_id=1, source_target_pairs={{24,16},{32,40},{25,17},{33,41},{26,18},{34,42},{27,19},{35,43},{2... | collective-permute-start | bytes 2654216 | tf_op jit(solution)/shard_map/over_f1/ppermute | solution.py:478
  265.4 2.0 collective-permute-done.14.refs_2_
  268.9 7.3 %last.1 = (f32[384,1152]{1,0:T(8,128)}, f32[384,1152]{1,0:T(8,128)}) custom-call(f32[2]{0:T(128)S(1)} %copy-done.13, bf16[384,1152]{1,0:T(8,128)(2,1)S(1)} %gate.7.refs_1_, bf16[384,1152]{1,0:T(8,128)(2,1)S(1)} %collective-permute-done.14.refs_2_, bf16[400,1152]{1,0:T(8,128)(2,1)S(1)} %copy-done.6, bf16[384,1152]{1,0:T(8,128)(2,1)S(1)} %copy-done.12, ...), custom_call_target="tpu_custom_call" | custom-call | flops 8000000000 | tf_op jit(solution)/shard_map/last/pallas_call | solution.py:35
  (63 shorter events, 14.4 us)
Async XLA Ops:
  5.0 13.1 %collective-permute-start.4 = (bf16[384,1152]{1,0:T(8,128)(2,1)}, bf16[384,1152]{1,0:T(8,128)(2,1)}, u32[]{:S(2)}, u32[]{:S(2)}) collective-permute-start(bf16[384,1152]{1,0:T(8,128)(2,1)} %get-tuple-element.22.refs_5_.refs_4_.refs_2_), channel_id=1, source_target_pairs={{0,2},{8,14},{2,4},{10,8},{4,6},{12,10},{6,0},{14,12},{1,3},{9,15}... | collective-permute-start | bytes 2654216 | tf_op jit(solution)/shard_map/one/ppermute | solution.py:381
  7.8 23.8 %collective-permute-start.7 = (bf16[384,1152]{1,0:T(8,128)(2,1)}, bf16[384,1152]{1,0:T(8,128)(2,1)}, u32[]{:S(2)}, u32[]{:S(2)}) collective-permute-start(bf16[384,1152]{1,0:T(8,128)(2,1)} %get-tuple-element.25.block_ref), channel_id=1, source_target_pairs={{16,32},{32,16},{17,33},{33,17},{18,34},{34,18},{19,35},{35,19},{2... | collective-permute-start | bytes 2654216 | tf_op jit(solution)/shard_map/mid/ppermute | solution.py:400
  10.9 48.8 %collective-permute-start.1 = (bf16[400,1152]{1,0:T(8,128)(2,1)}, bf16[400,1152]{1,0:T(8,128)(2,1)S(1)}, u32[]{:S(2)}, u32[]{:S(2)}) collective-permute-start(bf16[400,1152]{1,0:T(8,128)(2,1)} %get-tuple-element.21.refs_1_.refs_6_.refs_3_), channel_id=1, source_target_pairs={{0,1},{1,0},{2,3},{3,2},{4,5},{5,4},{6,7},{7,6},{8,9},{9,8},{10,11... | collective-permute-start | bytes 2764808 | tf_op jit(solution)/shard_map/other/ppermute | solution.py:28
  12.7 21.4 %collective-permute-start.8 = (bf16[384,1152]{1,0:T(8,128)(2,1)}, bf16[384,1152]{1,0:T(8,128)(2,1)S(1)}, u32[]{:S(2)}, u32[]{:S(2)}) collective-permute-start(bf16[384,1152]{1,0:T(8,128)(2,1)} %get-tuple-element.27), channel_id=1, source_target_pairs={{0,16},{16,0},{32,48},{48,32},{1,17},{17,1},{33,49},{49,33},{2,18}... | collective-permute-start | bytes 2654216 | tf_op jit(solution)/shard_map/near/ppermute | solution.py:398
  12.7 47.1 %collective-permute-start = (bf16[384,1152]{1,0:T(8,128)(2,1)}, bf16[384,1152]{1,0:T(8,128)(2,1)S(1)}, u32[]{:S(2)}, u32[]{:S(2)}) collective-permute-start(bf16[384,1152]{1,0:T(8,128)(2,1)} %get-tuple-element.20), channel_id=1, source_target_pairs={{0,0},{16,16},{32,32},{48,48},{56,8},{40,24},{24,40},{8,56},{1,1},... | collective-permute-start | bytes 2654216 | tf_op jit(solution)/shard_map/hop/ppermute | solution.py:391
  18.1 44.6 %collective-permute-start.5 = (bf16[384,1152]{1,0:T(8,128)(2,1)}, bf16[384,1152]{1,0:T(8,128)(2,1)}, u32[]{:S(2)}, u32[]{:S(2)}) collective-permute-start(bf16[384,1152]{1,0:T(8,128)(2,1)} %get-tuple-element.22.refs_5_.refs_4_.refs_2_), channel_id=1, source_target_pairs={{0,6},{8,10},{2,0},{10,12},{4,2},{12,14},{6,4},{14,8},{1,7},{9,11}... | collective-permute-start | bytes 2654216 | tf_op jit(solution)/shard_map/two/ppermute | solution.py:381
  31.7 42.0 %collective-permute-start.6 = (bf16[384,1152]{1,0:T(8,128)(2,1)}, bf16[384,1152]{1,0:T(8,128)(2,1)}, u32[]{:S(2)}, u32[]{:S(2)}) collective-permute-start(bf16[384,1152]{1,0:T(8,128)(2,1)} %collective-permute-done.4.refs_3_.refs_2_), channel_id=1, source_target_pairs={{0,2},{8,14},{2,4},{10,8},{4,6},{12,10},{6,0},{14,12},{1,3},{9,15}... | collective-permute-start | bytes 2654216 | tf_op jit(solution)/shard_map/opp/ppermute | solution.py:381
  35.3 24.5 %copy-start.8 = (bf16[384,1152]{1,0:T(8,128)(2,1)}, bf16[384,1152]{1,0:T(8,128)(2,1)S(1)}, u32[]{:S(2)}) copy-start(bf16[384,1152]{1,0:T(8,128)(2,1)S(1)} %collective-permute-done.8.after_ref.refs_7_) | copy-start | bytes 2654212
  36.2 45.7 %collective-permute-start.9 = (bf16[384,1152]{1,0:T(8,128)(2,1)}, bf16[384,1152]{1,0:T(8,128)(2,1)}, u32[]{:S(2)}, u32[]{:S(2)}) collective-permute-start(bf16[384,1152]{1,0:T(8,128)(2,1)} %copy-done.10), channel_id=1, source_target_pairs={{0,32},{32,0},{16,48},{48,16},{1,33},{33,1},{17,49},{49,17},{2,34}... | collective-permute-start | bytes 2654216 | tf_op jit(solution)/shard_map/far/ppermute | solution.py:402
  59.8 22.1 %collective-permute-start.2 = (bf16[384,1152]{1,0:T(8,128)(2,1)S(1)}, bf16[384,1152]{1,0:T(8,128)(2,1)}, u32[]{:S(2)}, u32[]{:S(2)}) collective-permute-start(bf16[384,1152]{1,0:T(8,128)(2,1)S(1)} %gate.4.refs_6_), channel_id=1, source_target_pairs={{48,64},{0,240},{8,72},{56,248},{112,128},{64,48},{72,136},{120,56... | collective-permute-start | bytes 2654216 | tf_op jit(solution)/shard_map/over_a/ppermute | solution.py:412
  61.4 20.5 %collective-permute-start.10 = (bf16[384,1152]{1,0:T(8,128)(2,1)S(1)}, bf16[384,1152]{1,0:T(8,128)(2,1)S(1)}, u32[]{:S(2)}, u32[]{:S(2)}) collective-permute-start(bf16[384,1152]{1,0:T(8,128)(2,1)S(1)} %gate.4.refs_6_), channel_id=1, source_target_pairs={{32,64},{16,240},{24,72},{40,248},{96,128},{80,48},{88,136},{104,5... | collective-permute-start | bytes 2654216 | tf_op jit(solution)/shard_map/over_b/ppermute | solution.py:412
  73.4 149.5 %collective-permute-start.12 = (bf16[384,1152]{1,0:T(8,128)(2,1)}, bf16[384,1152]{1,0:T(8,128)(2,1)S(1)}, u32[]{:S(2)}, u32[]{:S(2)}) collective-permute-start(bf16[384,1152]{1,0:T(8,128)(2,1)} %get-tuple-element.24.refs_4_), channel_id=1, source_target_pairs={{0,6},{8,10},{2,0},{10,12},{4,2},{12,14},{6,4},{14,8},{1,7},{9,11}... | collective-permute-start | bytes 2654216 | tf_op jit(solution)/shard_map/early/ppermute | solution.py:381
  79.2 143.8 %collective-permute-start.11 = (bf16[384,1152]{1,0:T(8,128)(2,1)}, bf16[384,1152]{1,0:T(8,128)(2,1)S(1)}, u32[]{:S(2)}, u32[]{:S(2)}) collective-permute-start(bf16[384,1152]{1,0:T(8,128)(2,1)} %get-tuple-element.30), channel_id=1, source_target_pairs={{0,2},{8,14},{2,4},{10,8},{4,6},{12,10},{6,0},{14,12},{1,3},{9,15}... | collective-permute-start | bytes 2654216 | tf_op jit(solution)/shard_map/carried/ppermute | solution.py:381
  231.5 9.8 %collective-permute-start.13 = (bf16[5,384,1152]{2,1,0:T(8,128)(2,1)}, bf16[5,384,1152]{2,1,0:T(8,128)(2,1)S(1)}, u32[]{:S(2)}, u32[]{:S(2)}) collective-permute-start(bf16[5,384,1152]{2,1,0:T(8,128)(2,1)} %copy-done.1), channel_id=1, source_target_pairs={{0,8},{8,0},{1,9},{9,1},{2,10},{10,2},{3,11},{11,3},{4,12},{12,4},... | collective-permute-start | bytes 13271048 | tf_op jit(solution)/shard_map/sib/ppermute | solution.py:28
  234.0 26.3 %collective-permute-start.3 = (bf16[384,1152]{1,0:T(8,128)(2,1)}, bf16[384,1152]{1,0:T(8,128)(2,1)S(1)}, u32[]{:S(2)}, u32[]{:S(2)}) collective-permute-start(bf16[384,1152]{1,0:T(8,128)(2,1)} %collective-permute-done.2.refs_10_), channel_id=1, source_target_pairs={{0,16},{48,32},{1,17},{49,33},{2,18},{50,34},{3,19},{51,35},{4,20}... | collective-permute-start | bytes 2654216 | tf_op jit(solution)/shard_map/over_f/ppermute | solution.py:465
  235.3 30.0 %collective-permute-start.15 = (bf16[384,1152]{1,0:T(8,128)(2,1)}, bf16[384,1152]{1,0:T(8,128)(2,1)}, u32[]{:S(2)}, u32[]{:S(2)}) collective-permute-start(bf16[384,1152]{1,0:T(8,128)(2,1)} %get-tuple-element.31.refs_2_), channel_id=1, source_target_pairs={{0,1},{1,0},{2,3},{3,2},{4,5},{5,4},{6,7},{7,6},{8,9},{9,8},{10,11... | collective-permute-start | bytes 2654216 | tf_op jit(solution)/shard_map/back/ppermute | solution.py:28
  235.4 30.0 %collective-permute-start.16 = (bf16[384,1152]{1,0:T(8,128)(2,1)}, bf16[384,1152]{1,0:T(8,128)(2,1)}, u32[]{:S(2)}, u32[]{:S(2)}) collective-permute-start(bf16[384,1152]{1,0:T(8,128)(2,1)} %add.1.after_ref.refs_7_), channel_id=1, source_target_pairs={{0,2},{8,14},{2,4},{10,8},{4,6},{12,10},{6,0},{14,12},{1,3},{9,15}... | collective-permute-start | bytes 2654216 | tf_op jit(solution)/shard_map/late/ppermute | solution.py:381
  243.4 23.9 %copy-start.6 = (bf16[400,1152]{1,0:T(8,128)(2,1)S(1)}, bf16[400,1152]{1,0:T(8,128)(2,1)}, u32[]{:S(2)}) copy-start(bf16[400,1152]{1,0:T(8,128)(2,1)} %get-tuple-element.21.refs_1_.refs_6_.refs_3_) | copy-start | bytes 2764804
  243.4 23.9 %copy-start.15 = (bf16[1,1,384,1152]{3,2,1,0:T(8,128)(2,1)S(1)}, bf16[1,1,384,1152]{3,2,1,0:T(8,128)(2,1)}, u32[]{:S(2)}) copy-start(bf16[1,1,384,1152]{3,2,1,0:T(8,128)(2,1)} %param.6) | copy-start | bytes 2654212
  243.4 23.9 %copy-start.16 = (bf16[1,1,384,1152]{3,2,1,0:T(8,128)(2,1)S(1)}, bf16[1,1,384,1152]{3,2,1,0:T(8,128)(2,1)}, u32[]{:S(2)}) copy-start(bf16[1,1,384,1152]{3,2,1,0:T(8,128)(2,1)} %param.5) | copy-start | bytes 2654212
  261.9 5.5 %copy-start.5 = (f32[384,1152]{1,0:T(8,128)S(1)}, f32[384,1152]{1,0:T(8,128)}, u32[]{:S(2)}) copy-start(f32[384,1152]{1,0:T(8,128)} %get-tuple-element.34.after_ref.refs_6_) | copy-start | bytes 5308420
  261.9 5.5 %copy-start.12 = (bf16[384,1152]{1,0:T(8,128)(2,1)S(1)}, bf16[384,1152]{1,0:T(8,128)(2,1)}, u32[]{:S(2)}) copy-start(bf16[384,1152]{1,0:T(8,128)(2,1)} %get-tuple-element.22.refs_5_.refs_4_.refs_2_) | copy-start | bytes 2654212
  261.9 5.5 %copy-start.13 = (f32[2]{0:T(128)S(1)}, f32[2]{0:T(128)}, u32[]{:S(2)}) copy-start(f32[2]{0:T(128)} %pad_maximum_fusion.refs_0_) | copy-start | bytes 28
  261.9 5.5 %collective-permute-start.14 = (bf16[384,1152]{1,0:T(8,128)(2,1)S(1)}, bf16[384,1152]{1,0:T(8,128)(2,1)S(1)}, u32[]{:S(2)}, u32[]{:S(2)}) collective-permute-start(bf16[384,1152]{1,0:T(8,128)(2,1)S(1)} %gate.7.refs_1_), channel_id=1, source_target_pairs={{24,16},{32,40},{25,17},{33,41},{26,18},{34,42},{27,19},{35,43},{2... | collective-permute-start | bytes 2654216 | tf_op jit(solution)/shard_map/over_f1/ppermute | solution.py:478
  (13 other events, 26.0 us)
where the time goes:
time: 277 us; the launch traced here: 276 us
  Pallas kernels  178 us (64%)
  waiting for transfers between devices  52.3 us (19%)
  starting transfers between devices  24.8 us (9%)
  local copies, waits for them, and re-layouts  18.3 us (7%)
    pallas_call x7, Pallas kernels, call(): pl.pallas_call(kernel, out_shape=[jax.ShapeDtypeStruct(s, d) for s, d in...  178 us
    ppermute x1, waiting for transfers between devices, local(): lax.ppermute(wrap, ('x', 'c'), [(turn(x, 0), turn(x, 0)) for x in range(4...  23 us
    unnamed x41, local copies, waits for them, and re-layouts  18.3 us
    ppermute x1, waiting for transfers between devices, local(): from_three = lax.ppermute(low, 'x', [(1, 2), (2, 1)])  12.8 us
    ppermute x6, starting transfers between devices, along_y(): return lax.ppermute(block, ('c', 'y'), pairs)  6.66 us
    ppermute x3, waiting for transfers between devices, ring(): return lax.ppermute(x, axis, [(i, (i + by) % size) for i in range(size)])  5.85 us
  transfers between devices with their start and end apart: 17, of which 7 were waited for; matrix products, arithmetic and copies ran while one was open for 2% of the time, Pallas kernels for 59%

commit v1 on v0

--- a/solution.py
+++ b/solution.py
@@ -37,7 +37,7 @@
         out_shape=[jax.ShapeDtypeStruct(s, d) for s, d in outs],
         in_specs=[SM] * smem + [space] * (len(args) - smem),
         out_specs=[ANY] * len(outs),
-        scratch_shapes=list(scratch) + [pltpu.SemaphoreType.DMA((32,))],
+        scratch_shapes=list(scratch) + [pltpu.SemaphoreType.DMA((40,))],
         cost_estimate=pl.CostEstimate(flops=flops, bytes_accessed=0, transcendentals=0),
         compiler_params=pltpu.CompilerParams(vmem_limit_bytes=limit * 2**20),
         name=name,
@@ -83,7 +83,7 @@
 
 
 def unit_kernel(
-    copies, ids_ref, cap_ref, pic_ref, text_out, image_out, wrap_out, even_out, low_out,
+    copies, ids_ref, cap_ref, pic_ref, text_out, image_out, wrap_out, even_out, low_out, mid_out,
     cap, pic, text, image, wrap, even, low,
 ):
     x = lax.axis_index("x")
@@ -114,7 +114,7 @@
         wrap[at, :] = jnp.where(x >= 2, t, i)
         even[at, :] = jnp.where(lax.rem(x, 2) == 0, t, i)
         low[at, :] = jnp.where(x < 2, t, i)
-        for src, dst in ((text, text_out), (wrap, wrap_out), (even, even_out), (low, low_out)):
+        for src, dst in ((text, text_out), (wrap, wrap_out), (even, even_out), (low, low_out), (low, mid_out)):
             leave.append(copies.go(src.at[at], dst.at[at]))
         if k == 0:
             leave.append(copies.go(image.at[at], image_out.at[at]))
@@ -175,28 +175,32 @@
     early_out, late_out, gt_out, wt_out, x_scr, near, far, t_scr, early, late, gt, wt,
 ):
     images = fetch_images(copies, image_ref, other_ref, x_scr, near, far)
-    texts = [copies.go(ref, t_scr.at[k]) for k, ref in enumerate((one_ref, two_ref, text_ref))]
+    order = (2, 1, 0)
+    refs = (one_ref, two_ref, text_ref)
+    texts = [copies.go(refs[order[0]], t_scr.at[order[0]])]
     owner = owners()
     for copy in images:
         copy.wait()
     leave = []
-    for k in range(3):
-        texts[k].wait()
+    for n, k in enumerate(order):
+        texts[n].wait()
+        if n == 0:
+            texts += [copies.go(refs[m], t_scr.at[m]) for m in order[1:]]
+        at = pl.ds(k * ROWS, ROWS)
         hard_weights(t_scr[k], x_scr, wt, k * ROWS, par_ref, near, far, owner[k], k == 2)
-        p = nn(wt[pl.ds(k * ROWS, ROWS), :], x_scr[...])
-        if k == 0:
-            early[...] = p.astype(BF16)
-        else:
-            (late, gt)[k - 1][...] = p
-        src, dst = ((early, early_out), (late, late_out), (gt, gt_out))[k]
-        leave.append(copies.go(src, dst))
-    leave.append(copies.go(wt, wt_out))
+        leave.append(copies.go(wt.at[at], wt_out.at[at]))
+        dst, out = ((early, early_out), (late, late_out), (gt, gt_out))[k]
+        for h in range(2):
+            part = pl.ds(h * HALF, HALF)
+            p = nn(wt[pl.ds(k * ROWS + h * HALF, HALF), :], x_scr[...])
+            dst[part, :] = p.astype(dst.dtype)
+            leave.append(copies.go(dst.at[part], out.at[part]))
     for copy in leave:
         copy.wait()
 
 
 def opposite_kernel(
-    copies, par_ref, image_ref, other_ref, opp_ref, after_ref, then_ref, return_out, wt_out,
+    copies, par_ref, image_ref, other_ref, opp_ref, after_ref, then_ref, again_ref, return_out, wt_out,
     x_scr, near, far, text, back, wt,
 ):
     images = fetch_images(copies, image_ref, other_ref, x_scr, near, far)
@@ -205,45 +209,66 @@
         copy.wait()
     hard_weights(text[...], x_scr, wt, 0, par_ref, near, far, owners()[3], False)
     leave = [copies.go(wt, wt_out)]
-    back[...] = nn(wt[...], x_scr[...]).astype(BF16)
-    leave.append(copies.go(back, return_out))
+    for h in range(2):
+        part = pl.ds(h * HALF, HALF)
+        back[part, :] = nn(wt[part, :], x_scr[...]).astype(BF16)
+        leave.append(copies.go(back.at[part], return_out.at[part]))
     for copy in leave:
         copy.wait()
 
 
 def image_kernel(
-    copies, wt3_ref, wt_ref, one_ref, two_ref, text_ref, opp_ref, image_ref, from_one,
-    from_two, from_three, aw, bw, far_out, near_out, own_out, w_scr, t_scr, far, near,
-):
-    come = [
-        copies.go(wt3_ref, w_scr.at[pl.ds(0, 3 * ROWS)]),
-        copies.go(wt_ref, w_scr.at[pl.ds(3 * ROWS, ROWS)]),
-    ]
+    copies, wt3_ref, wt_ref, one_ref, two_ref, text_ref, opp_ref, after_ref, then_ref,
+    again_ref, far_out, near_out, w_scr, t_scr, far, near,
+):
+    come = [copies.go(wt3_ref, w_scr.at[pl.ds(0, 3 * ROWS)])]
     for k, ref in enumerate((one_ref, two_ref, text_ref, opp_ref)):
         come.append(copies.go(ref, t_scr.at[pl.ds(k * ROWS, ROWS)]))
-    image = image_ref.at[pl.ds(0, ROWS)]
-    leave = [copies.pick(lax.axis_index("c") == 0, text_ref, image, own_out.at[0])]
+    come.append(copies.go(wt_ref, w_scr.at[pl.ds(3 * ROWS, ROWS)]))
+    for copy in come[:3]:
+        copy.wait()
+    pair = pl.ds(0, 2 * ROWS)
+    near[...] = tn(w_scr[pair, :ROWS], t_scr[pair, :])
+    for copy in come[3:]:
+        copy.wait()
+    rest = pl.ds(2 * ROWS, 2 * ROWS)
+    near[...] += tn(w_scr[rest, :ROWS], t_scr[rest, :])
+    leave = [copies.go(near, near_out)]
+    for h in range(2):
+        part = pl.ds(h * HALF, HALF)
+        far[part, :] = tn(w_scr[:, ROWS:][:, h * HALF : (h + 1) * HALF], t_scr[...]).astype(BF16)
+        leave.append(copies.go(far.at[part], far_out.at[part]))
+    for copy in leave:
+        copy.wait()
+
+
+def bundle_kernel(
+    copies, text_ref, image_ref, from_one, from_two, from_three, aw, bw, after_ref, out_ref, own
+):
     x = lax.axis_index("x")
     inner = jnp.logical_or(x == 1, x == 2)
-    for k, ref in enumerate((from_one, from_two)):
-        leave.append(copies.go(ref, own_out.at[k + 1]))
-    leave.append(copies.pick(inner, from_three, aw, own_out.at[3]))
-    leave.append(copies.go(bw, own_out.at[4]))
-    for copy in come:
-        copy.wait()
-    far[...] = tn(w_scr[:, ROWS:], t_scr[...]).astype(BF16)
-    leave.append(copies.go(far, far_out))
-    near[...] = tn(w_scr[:, :ROWS], t_scr[...])
-    leave.append(copies.go(near, near_out))
-    for copy in leave:
-        copy.wait()
-
-
-def attend(mine, scr, w_scr, par_ref, count):
-    for j in range(count * 3 // 2):
-        at = pl.ds(j * 256, 256)
+    image = image_ref.at[pl.ds(0, ROWS)]
+    come = [
+        copies.pick(lax.axis_index("c") == 0, text_ref, image, own.at[0]),
+        copies.go(from_one, own.at[1]),
+        copies.go(from_two, own.at[2]),
+        copies.pick(inner, from_three, aw, own.at[3]),
+        copies.go(bw, own.at[4]),
+    ]
+    leave = []
+    for k, copy in enumerate(come):
+        copy.wait()
+        leave.append(copies.go(own.at[k], out_ref.at[k]))
+    for copy in leave:
+        copy.wait()
+
+
+def attend(mine, scr, w_scr, par_ref, first):
+    for j in range(3):
+        at = pl.ds(first * ROWS + j * 256, 256)
         w_scr[:, at] = weights(nt(mine, scr[at, :]), par_ref).astype(BF16)
-    return nn(w_scr[:, : count * ROWS], scr[: count * ROWS, :])
+    both = pl.ds(first * ROWS, 2 * ROWS)
+    return nn(w_scr[:, both], scr[both, :])
 
 
 def cycle_kernel(
@@ -252,9 +277,8 @@
 ):
     x, core = lax.axis_index("x"), lax.axis_index("c")
     come = []
-    for low, mine_ref, mine, grad_ref, grad, scr in (
-        (True, image_ref, image, gi_ref, gi, t_scr),
-        (False, text_ref, text, gt_ref, gt, i_scr),
+    for low, mine_ref, mine, scr in (
+        (True, image_ref, image, t_scr), (False, text_ref, text, i_scr)
     ):
         d = x if low else 3 - x
         e = core if low else 1 - core
@@ -265,34 +289,54 @@
             return jnp.where(i >= 0, inside, beyond)
 
         swapped = jnp.logical_and(d == 0, e == 1)
-        here = [
-            copies.go(mine_ref.at[pl.ds(0, ROWS)], mine),
-            copies.go(own.at[place(d - 1, 3)], slot(0)),
-            copies.go(own.at[place(d - 2, 4)], slot(1)),
-            copies.go(sib.at[place(d - 1 + e, 3)], slot(2)),
-            copies.go(sib.at[place(d - 2 + e, jnp.where(swapped, 3, 4))], slot(3)),
-        ]
-        here.append(copies.go(grad_ref, grad))
-        come.append(here)
+        come.append([
+            lambda a=mine_ref, b=mine: copies.go(a.at[pl.ds(0, ROWS)], b),
+            lambda a=own.at[place(d - 1, 3)], b=slot(0): copies.go(a, b),
+            lambda a=own.at[place(d - 2, 4)], b=slot(1): copies.go(a, b),
+            lambda a=sib.at[place(d - 1 + e, 3)], b=slot(2): copies.go(a, b),
+            lambda a=sib.at[place(d - 2 + e, jnp.where(swapped, 3, 4))], b=slot(3): copies.go(a, b),
+        ])
+    waiting = [start() for start in come[0][:5]]
     leave = []
-    for here, mine, grad, scr, out in (
-        (come[0], image, gi, t_scr, gi_out),
-        (come[1], text, gt, i_scr, gt_out),
+    for side, (mine, grad, scr, out) in enumerate(
+        ((image, gi, t_scr, gi_out), (text, gt, i_scr, gt_out))
     ):
-        for copy in here:
+        for copy in waiting[:3]:
             copy.wait()
-        grad[...] += attend(mine[...], scr, w_scr, par_ref, 4)
-        leave.append(copies.go(grad, out))
+        total = copies.go(gi_ref if side == 0 else gt_ref, grad)
+        following = [start() for start in come[1][:3]] if side == 0 else []
+        p = attend(mine[...], scr, w_scr, par_ref, 0)
+        total.wait()
+        grad[...] += p
+        for copy in waiting[3:]:
+            copy.wait()
+        if side == 0:
+            following += [start() for start in come[1][3:5]]
+        for h in range(2):
+            part = pl.ds(h * HALF, HALF)
+            if h == 0:
+                p = attend(mine[...], scr, w_scr, par_ref, 2)
+            grad[part, :] += p[h * HALF : (h + 1) * HALF]
+            leave.append(copies.go(grad.at[part], out.at[part]))
+        waiting = following
     for copy in leave:
         copy.wait()
 
 
 def add_kernel(copies, late_ref, return_ref, after_ref, then_ref, out_ref, late, back, out):
-    come = [copies.go(late_ref, late), copies.go(return_ref, back)]
-    for copy in come:
-        copy.wait()
-    out[...] = (late[...] + back[...].astype(F32)).astype(BF16)
-    copies.go(out, out_ref).wait()
+    parts = [pl.ds(k * BLOCK, BLOCK) for k in range(3)]
+    come = [
+        (copies.go(late_ref.at[at], late.at[at]), copies.go(return_ref.at[at], back.at[at]))
+        for at in parts
+    ]
+    leave = []
+    for at, pair in zip(parts, come):
+        for copy in pair:
+            copy.wait()
+        out[at, :] = (late[at, :] + back[at, :].astype(F32)).astype(BF16)
+        leave.append(copies.go(out.at[at], out_ref.at[at]))
+    for copy in leave:
+        copy.wait()
 
 
 def gate_kernel(block_ref, after_ref, out_ref):
@@ -313,30 +357,38 @@
     scr, w_scr, mine, more, pic, gi, back, cap, gt, early, late,
 ):
     x = lax.axis_index("x")
+    inner = jnp.logical_or(x == 1, x == 2)
     come = [
-        copies.go(f, scr.at[pl.ds(0, ROWS)]),
-        copies.go(f1, scr.at[pl.ds(ROWS, ROWS)]),
-        copies.pick(x <= 1, image_ref.at[pl.ds(0, ROWS)], text_ref, mine),
+        copies.of(f, scr.at[pl.ds(0, ROWS)]),
+        copies.of(f1, scr.at[pl.ds(ROWS, ROWS)]),
+        copies.of(text_ref, mine),
     ]
+    for copy in come[:2]:
+        pl.when(inner)(copy.start)
+    pl.when(x == 2)(come[2].start)
+    first = pltpu.make_async_copy(
+        image_ref.at[pl.ds(0, ROWS)], mine, copies.sems.at[copies.count - 1]
+    )
+    pl.when(x == 1)(first.start)
+    parts = [pl.ds(k * BLOCK, BLOCK) for k in range(3)]
     rest = [
-        copies.go(src, dst)
-        for src, dst in (
+        [copies.go(src.at[at], dst.at[at]) for src, dst in (
             (pic_ref, pic), (gi_ref, gi), (back_ref, back), (cap_ref, cap), (gt_ref, gt),
             (early_ref, early), (late_ref, late),
-        )
+        )]
+        for at in parts
     ]
-    for copy in come:
-        copy.wait()
-
-    @pl.when(jnp.logical_or(x == 1, x == 2))
+
+    @pl.when(inner)
     def _():
-        more[...] = attend(mine[...], scr, w_scr, par_ref, 2)
-
-    for copy in rest:
-        copy.wait()
+        for copy in come:
+            copy.wait()
+        more[...] = attend(mine[...], scr, w_scr, par_ref, 0)
+
     leave = []
-    for k in range(3):
-        at = pl.ds(k * BLOCK, BLOCK)
+    for at, here in zip(parts, rest):
+        for copy in here:
+            copy.wait()
         g = gi[at, :] + back[at, :].astype(F32)
         g = jnp.where(x == 1, g + more[at, :], g)
         gi[at, :] = through_norm(pic[at, :], g)
@@ -353,10 +405,10 @@
     return pl.pallas_call(
         gate_kernel,
         out_shape=jax.ShapeDtypeStruct(block.shape, block.dtype),
-        in_specs=[FREE, FREE],
-        out_specs=FREE,
+        in_specs=[ANY, ANY],
+        out_specs=ANY,
         input_output_aliases={0: 0},
-        compiler_params=pltpu.CompilerParams(vmem_limit_bytes=2**20),
+        compiler_params=pltpu.CompilerParams(vmem_limit_bytes=60 * 2**20),
         name="gate",
     )(block, after)
 
@@ -365,9 +417,9 @@
     pics, caps = pictures[0, 0], captions[0, 0]
     par = jnp.stack([sharpness, offset])
     counts = [vm(16), vm(16)]
-    text, image, wrap, even, low = call(
+    text, image, wrap, even, low, middle = call(
         unit_kernel,
-        [WHOLE, ((ROWS + 16, WIDTH), BF16), WHOLE, WHOLE, WHOLE],
+        [WHOLE, ((ROWS + 16, WIDTH), BF16)] + [WHOLE] * 4,
         (tile_numbers[0, 0].T, caps, pics),
         [vm(ROWS), vm(ROWS), vm(ROWS), vm(ROWS + 16), vm(ROWS), vm(ROWS), vm(ROWS)],
         "unit",
@@ -387,39 +439,32 @@
         other = ring(image, "zl", 1)
     with jax.named_scope("two"):
         text_two = along_y(text, -1)
-    with jax.named_scope("hop"):
-        hop = lax.ppermute(
-            wrap,
-            ("x", "c"),
-            [(turn(x, 0), turn(x, 0)) for x in range(4)]
-            + [(turn(a, 1), turn(b, 1)) for a, b in ((3, 0), (2, 1), (1, 2), (0, 3))],
-        )
     with jax.named_scope("near"):
         from_one = lax.ppermute(even, "x", [(0, 1), (1, 0), (2, 3), (3, 2)])
     with jax.named_scope("mid"):
-        from_three = lax.ppermute(low, "x", [(1, 2), (2, 1)])
+        from_three = lax.ppermute(middle, "x", [(1, 2), (2, 1)])
     with jax.named_scope("far"):
         from_two = lax.ppermute(gate(low, from_one), "x", [(0, 2), (2, 0), (1, 3), (3, 1)])
     with jax.named_scope("opp"):
         text_opp = along_y(text_one, 1)
-    hop = gate(hop, other)
+    wrap = gate(wrap, other)
 
     def over(pairs):
         sends = []
         for z in range(4):
-            for a, b, c, d in pairs:
-                sends.append((z * 8 + turn(a, c), (z + d) % 4 * 8 + turn(b, c)))
-        return lax.ppermute(hop, GROUP, sends)
+            for a, b, d in pairs:
+                sends += [(z * 8 + turn(a, c), (z + d) % 4 * 8 + turn(b, c)) for c in range(2)]
+        return lax.ppermute(wrap, GROUP, sends)
 
     with jax.named_scope("over_a"):
-        over_a = over([(3, 0, 0, 1), (0, 3, 0, -1), (0, 0, 1, 1), (3, 3, 1, -1)])
+        over_a = over([(3, 0, 1), (0, 3, -1)])
     with jax.named_scope("over_b"):
-        over_b = over([(2, 0, 0, 1), (1, 3, 0, -1), (1, 0, 1, 1), (2, 3, 1, -1)])
+        over_b = over([(2, 0, 1), (1, 3, -1)])
 
     part_early, part_late, grad_text, wt3 = call(
         hard_kernel,
         [WHOLE, WHOLE32, WHOLE32, ((3 * ROWS, 2 * ROWS), BF16)],
-        (par, image, other, text_one, text_two, text, hop),
+        (par, image, other, text_one, text_two, text, from_one),
         [vm(2 * ROWS), *counts, pltpu.VMEM((3, ROWS, WIDTH), BF16), vm(ROWS),
          vm(ROWS, dtype=F32), vm(ROWS, dtype=F32), vm(3 * ROWS, 2 * ROWS)],
         "hard",
@@ -430,27 +475,33 @@
     part_opp, wt = call(
         opposite_kernel,
         [WHOLE, ((ROWS, 2 * ROWS), BF16)],
-        (par, image, other, text_opp, part_early, from_three),
+        (par, image, other, text_opp, part_early, from_two, from_three),
         [vm(2 * ROWS), *counts, vm(ROWS), vm(ROWS), vm(ROWS, 2 * ROWS)],
         "opposite",
         1,
     )
     with jax.named_scope("carried"):
         carried = along_y(part_opp, 1)
-    grad_far, grad_image, own = call(
+    grad_far, grad_image = call(
         image_kernel,
-        [WHOLE, WHOLE32, ((5, ROWS, WIDTH), BF16)],
-        (wt3, wt, text_one, text_two, text, text_opp, image, from_one, from_two, from_three,
-         over_a, over_b),
+        [WHOLE, WHOLE32],
+        (wt3, wt, text_one, text_two, text, text_opp, from_one, from_two, from_three),
         [vm(4 * ROWS, 2 * ROWS), vm(4 * ROWS), vm(ROWS), vm(ROWS, dtype=F32)],
         "image_side",
     )
+    own = call(
+        bundle_kernel,
+        [((5, ROWS, WIDTH), BF16)],
+        (text, image, from_one, from_two, from_three, over_a, over_b, grad_far),
+        [pltpu.VMEM((5, ROWS, WIDTH), BF16)],
+        "bundle",
+    )[0]
     with jax.named_scope("back"):
         grad_back = ring(grad_far, "zl", 1)
     part_late = call(
         add_kernel,
         [WHOLE],
-        (part_late, carried, grad_far, early),
+        (part_late, carried, own, early),
         [vm(ROWS, dtype=F32), vm(ROWS), vm(ROWS)],
         "add",
         flops=1,
@@ -459,7 +510,7 @@
         late = along_y(part_late, 1)
 
     with jax.named_scope("sib"):
-        sib = ring(gate(own, part_late), "c", 1)
+        sib = ring(own, "c", 1)
 
     with jax.named_scope("over_f"):
         over_f = lax.ppermute(over_a, "x", [(0, 1), (3, 2)])
@@ -487,8 +538,6 @@
          vm(ROWS, dtype=F32), vm(ROWS), vm(ROWS), vm(ROWS, dtype=F32), vm(ROWS), vm(ROWS)],
         "last",
         1,
-        FREE,
-        24,
     )
     return (image_grad[None, None], text_grad[None, None])
 

time: 277 us -> 161 us (0.58)
  Pallas kernels: 178 us -> 53.9 us
  starting transfers between devices: 24.8 us -> 38.3 us
  local copies, waits for them, and re-layouts: 18.3 us -> 6.73 us
  waiting for transfers between devices: 52.3 us -> 58.3 us
    pallas_call x7 -> x8, Pallas kernels: 178 us -> 53.9 us  [call(): pl.pallas_call(kernel, out_shape=[jax.ShapeDtypeStruct(s, d) for s, d in...]
    ppermute x4 -> x3, waiting for transfers between devices: 35.7 us -> 0.01 us  [the longest x2 0.01 us: over(): return lax.ppermute(wrap, GROUP, sends)]
    ppermute x1, waiting for transfers between devices: 0.01 us -> 27.5 us  [local(): lax.ppermute(gate(low, from_one), 'x', [(0, 2), (2, 0), (1, 3), (3, 1)])]
    ppermute x6, waiting for transfers between devices: 3 us -> 16.5 us  [along_y(): return lax.ppermute(block, ('c', 'y'), pairs)]
    ppermute x1, waiting for transfers between devices: 0.49 us -> 12.1 us  [local(): from_one = lax.ppermute(even, 'x', [(0, 1), (1, 0), (2, 3), (3, 2)])]
    unnamed x41 -> x22, local copies, waits for them, and re-layouts: 18.3 us -> 6.73 us
    ppermute x4 -> x3, starting transfers between devices: 8.52 us -> 14.7 us  [the longest x2 10.9 us: over(): return lax.ppermute(wrap, GROUP, sends)]
    ppermute x3, waiting for transfers between devices: 5.85 us -> 0.01 us  [ring(): return lax.ppermute(x, axis, [(i, (i + by) % size) for i in range(size)])]
  transfers between devices with their start and end apart: 17 -> 16, of which waited for: 7 -> 5; matrix products, arithmetic and copies ran while one was open for 2% -> 0% of each run, Pallas kernels for 59% -> 24%
where the time goes in v1:
time: 161 us; the launch traced here: 160 us
  waiting for transfers between devices  58.3 us (36%)
  Pallas kernels  53.9 us (33%)
  starting transfers between devices  38.3 us (24%)
  local copies, waits for them, and re-layouts  6.73 us (4%)
  between operations  2.33 us (1%)
    pallas_call x8, Pallas kernels, call(): pl.pallas_call(kernel, out_shape=[jax.ShapeDtypeStruct(s, d) for s, d in...  53.9 us
    ppermute x1, waiting for transfers between devices, local(): lax.ppermute(gate(low, from_one), 'x', [(0, 2), (2, 0), (1, 3), (3, 1)])  27.5 us
    ppermute x6, waiting for transfers between devices, along_y(): return lax.ppermute(block, ('c', 'y'), pairs)  16.5 us
    ppermute x1, waiting for transfers between devices, local(): from_one = lax.ppermute(even, 'x', [(0, 1), (1, 0), (2, 3), (3, 2)])  12.1 us
    ppermute x6, starting transfers between devices, along_y(): return lax.ppermute(block, ('c', 'y'), pairs)  11.5 us
    ppermute x2, starting transfers between devices, over(): return lax.ppermute(wrap, GROUP, sends)  10.9 us
    ppermute x3, starting transfers between devices, ring(): return lax.ppermute(x, axis, [(i, (i + by) % size) for i in range(size)])  7.31 us
    unnamed x22, local copies, waits for them, and re-layouts  6.73 us
  transfers between devices with their start and end apart: 16, of which 5 were waited for; matrix products, arithmetic and copies ran while one was open for 0% of the time, Pallas kernels for 24%

profile of v1, /device:TPU:3, one launch (start us, length us, event | category | flops | bytes accessed | tf_op | source)
XLA Modules:
  0.0 160.2 jit_solution(9936972934992606324)
XLA Ops:
  0.6 4.7 %unit.1 = (bf16[384,1152]{1,0:T(8,128)(2,1)}, bf16[400,1152]{1,0:T(8,128)(2,1)}, bf16[384,1152]{1,0:T(8,128)(2,1)}, bf16[384,1152]{1,0:T(8,128)(2,1)}, bf16[384,...) custom-call(s32[2,8]{1,0:T(2,128)} %bitcast.15, bf16[384,1152]{1,0:T(8,128)(2,1)} %bitcast.11, bf16[384,1152]{1,0:T(8,128)(2,1)} %bitcast.13), custom_call_target="tpu_custom_call" | custom-call | flops 8000000000 | tf_op jit(solution)/shard_map/unit/pallas_call | solution.py:35
  5.5 3.0 %collective-permute-start.7 = (bf16[384,1152]{1,0:T(8,128)(2,1)}, bf16[384,1152]{1,0:T(8,128)(2,1)}, u32[]{:S(2)}, u32[]{:S(2)}) collective-permute-start(bf16[384,1152]{1,0:T(8,128)(2,1)} %get-tuple-element.22.refs_5_.refs_4_.refs_0_.refs_2_), channel_id=1, source_target_pairs={{0,2},{8,14},{2,4},{10,8},{4,6},{12,10},{6,0},{14,12},{1,3},{9,15}... | collective-permute-start | bytes 2654216 | tf_op jit(solution)/shard_map/one/ppermute | solution.py:433
  8.5 1.6 %collective-permute-start = (bf16[400,1152]{1,0:T(8,128)(2,1)}, bf16[400,1152]{1,0:T(8,128)(2,1)S(1)}, u32[]{:S(2)}, u32[]{:S(2)}) collective-permute-start(bf16[400,1152]{1,0:T(8,128)(2,1)} %get-tuple-element.21.refs_1_.refs_3_), channel_id=1, source_target_pairs={{0,1},{1,0},{2,3},{3,2},{4,5},{5,4},{6,7},{7,6},{8,9},{9,8},{10,11... | collective-permute-start | bytes 2764808 | tf_op jit(solution)/shard_map/other/ppermute | solution.py:28
  10.1 3.8 %collective-permute-start.5 = (bf16[384,1152]{1,0:T(8,128)(2,1)}, bf16[384,1152]{1,0:T(8,128)(2,1)}, u32[]{:S(2)}, u32[]{:S(2)}) collective-permute-start(bf16[384,1152]{1,0:T(8,128)(2,1)} %get-tuple-element.25), channel_id=1, source_target_pairs={{16,32},{32,16},{17,33},{33,17},{18,34},{34,18},{19,35},{35,19},{2... | collective-permute-start | bytes 2654216 | tf_op jit(solution)/shard_map/mid/ppermute | solution.py:445
  13.9 12.1 %collective-permute-done.3.after_ref.refs_6_.refs_2_ = bf16[384,1152]{1,0:T(8,128)(2,1)S(1)} collective-permute-done((bf16[384,1152]{1,0:T(8,128)(2,1)}, bf16[384,1152]{1,0:T(8,128)(2,1)S(1)}, u32[]{:S(2)}, u32[]{:S(2)}) %collective-permute-start.3) | collective-permute-done | bytes 884768 | tf_op jit(solution)/shard_map/near/ppermute | solution.py:443
  26.9 2.1 %collective-permute-start.4 = (bf16[384,1152]{1,0:T(8,128)(2,1)}, bf16[384,1152]{1,0:T(8,128)(2,1)S(1)}, u32[]{:S(2)}, u32[]{:S(2)}) collective-permute-start(bf16[384,1152]{1,0:T(8,128)(2,1)} %gate.4), channel_id=1, source_target_pairs={{0,32},{32,0},{16,48},{48,16},{1,33},{33,1},{17,49},{49,17},{2,34}... | collective-permute-start | bytes 2654216 | tf_op jit(solution)/shard_map/far/ppermute | solution.py:447
  29.1 2.7 %collective-permute-start.9 = (bf16[384,1152]{1,0:T(8,128)(2,1)}, bf16[384,1152]{1,0:T(8,128)(2,1)}, u32[]{:S(2)}, u32[]{:S(2)}) collective-permute-start(bf16[384,1152]{1,0:T(8,128)(2,1)} %collective-permute-done.7.refs_3_.refs_2_), channel_id=1, source_target_pairs={{0,2},{8,14},{2,4},{10,8},{4,6},{12,10},{6,0},{14,12},{1,3},{9,15}... | collective-permute-start | bytes 2654216 | tf_op jit(solution)/shard_map/opp/ppermute | solution.py:433
  35.4 10.2 %collective-permute-start.6 = (bf16[384,1152]{1,0:T(8,128)(2,1)}, bf16[384,1152]{1,0:T(8,128)(2,1)S(1)}, u32[]{:S(2)}, u32[]{:S(2)}) collective-permute-start(bf16[384,1152]{1,0:T(8,128)(2,1)} %gate.3), channel_id=1, source_target_pairs={{32,64},{40,72},{16,240},{24,248},{96,128},{104,136},{80,48},{88,5... | collective-permute-start | bytes 2654216 | tf_op jit(solution)/shard_map/over_b/ppermute | solution.py:457
  45.6 10.3 %hard.1 = (bf16[384,1152]{1,0:T(8,128)(2,1)}, f32[384,1152]{1,0:T(8,128)}, f32[384,1152]{1,0:T(8,128)}, bf16[1152,768]{1,0:T(8,128)(2,1)}) custom-call(f32[2]{0:T(128)} %pad_maximum_fusion.refs_0_, bf16[400,1152]{1,0:T(8,128)(2,1)} %get-tuple-element.21.refs_1_.refs_3_, bf16[400,1152]{1,0:T(8,128)(2,1)} %copy-done.1, ...), custom_call_target="tpu_custom_call" | custom-call | flops 8000000000 | tf_op jit(solution)/shard_map/hard/pallas_call | solution.py:35
  55.9 27.5 %collective-permute-done.4.refs_5_.refs_7_.refs_3_ = bf16[384,1152]{1,0:T(8,128)(2,1)S(1)} collective-permute-done((bf16[384,1152]{1,0:T(8,128)(2,1)}, bf16[384,1152]{1,0:T(8,128)(2,1)S(1)}, u32[]{:S(2)}, u32[]{:S(2)}) %collective-permute-start.4) | collective-permute-done | bytes 884768 | tf_op jit(solution)/shard_map/far/ppermute | solution.py:447
  84.4 5.8 %opposite.1 = (bf16[384,1152]{1,0:T(8,128)(2,1)}, bf16[384,768]{1,0:T(8,128)(2,1)}) custom-call(f32[2]{0:T(128)} %pad_maximum_fusion.refs_0_, bf16[400,1152]{1,0:T(8,128)(2,1)} %get-tuple-element.21.refs_1_.refs_3_, bf16[400,1152]{1,0:T(8,128)(2,1)} %copy-done.1, bf16[384,1152]{1,0:T(8,128)(2,1)} %collective-permute-done.9.refs_3_.refs_5_, ...), custom_call_target="tpu_custom_call" | custom-call | flops 8000000000 | tf_op jit(solution)/shard_map/opposite/pallas_call | solution.py:35
  90.2 6.7 %image_side.1 = (bf16[384,1152]{1,0:T(8,128)(2,1)}, f32[384,1152]{1,0:T(8,128)}) custom-call(bf16[1152,768]{1,0:T(8,128)(2,1)} %get-tuple-element.26.refs_0_, bf16[384,768]{1,0:T(8,128)(2,1)} %get-tuple-element.28.refs_1_, bf16[384,1152]{1,0:T(8,128)(2,1)} %collective-permute-done.7.refs_3_.refs_2_, ...), custom_call_target="tpu_custom_call" | custom-call | flops 8000000000 | tf_op jit(solution)/shard_map/image_side/pallas_call | solution.py:35
  98.2 3.9 %bundle.1.refs_2_.refs_3_ = bf16[5,384,1152]{2,1,0:T(8,128)(2,1)} custom-call(bf16[384,1152]{1,0:T(8,128)(2,1)} %get-tuple-element.22.refs_5_.refs_4_.refs_0_.refs_2_, bf16[400,1152]{1,0:T(8,128)(2,1)} %get-tuple-element.21.refs_1_.refs_3_, bf16[384,1152]{1,0:T(8,128)(2,1)} %copy-done.4, bf16[384,1152]{1,0:T(8,128)(2,1)} %copy-done.6, ...), custom_call_target="tpu_custom_call" | custom-call | flops 8000000000 | tf_op jit(solution)/shard_map/bundle/pallas_call | solution.py:35
  102.0 3.7 %collective-permute-start.10 = (bf16[5,384,1152]{2,1,0:T(8,128)(2,1)}, bf16[5,384,1152]{2,1,0:T(8,128)(2,1)}, u32[]{:S(2)}, u32[]{:S(2)}) collective-permute-start(bf16[5,384,1152]{2,1,0:T(8,128)(2,1)} %bundle.1.refs_2_.refs_3_), channel_id=1, source_target_pairs={{0,8},{8,0},{1,9},{9,1},{2,10},{10,2},{3,11},{11,3},{4,12},{12,4},... | collective-permute-start | bytes 13271048 | tf_op jit(solution)/shard_map/sib/ppermute | solution.py:28
  107.1 1.5 collective-permute-start.11
  109.8 1.9 %collective-permute-start.14 = (bf16[384,1152]{1,0:T(8,128)(2,1)}, bf16[384,1152]{1,0:T(8,128)(2,1)S(1)}, u32[]{:S(2)}, u32[]{:S(2)}) collective-permute-start(bf16[384,1152]{1,0:T(8,128)(2,1)} %get-tuple-element.29.refs_7_), channel_id=1, source_target_pairs={{0,1},{1,0},{2,3},{3,2},{4,5},{5,4},{6,7},{7,6},{8,9},{9,8},{10,11... | collective-permute-start | bytes 2654216 | tf_op jit(solution)/shard_map/back/ppermute | solution.py:28
  111.7 13.6 %collective-permute-done.12.refs_3_.refs_8_.refs_10_ = bf16[384,1152]{1,0:T(8,128)(2,1)S(1)} collective-permute-done((bf16[384,1152]{1,0:T(8,128)(2,1)}, bf16[384,1152]{1,0:T(8,128)(2,1)S(1)}, u32[]{:S(2)}, u32[]{:S(2)}) %collective-permute-start.12) | collective-permute-done | bytes 884768 | tf_op jit(solution)/shard_map/early/ppermute | solution.py:433
  125.3 2.9 %collective-permute-done.11.refs_1_ = bf16[384,1152]{1,0:T(8,128)(2,1)S(1)} collective-permute-done((bf16[384,1152]{1,0:T(8,128)(2,1)}, bf16[384,1152]{1,0:T(8,128)(2,1)S(1)}, u32[]{:S(2)}, u32[]{:S(2)}) %collective-permute-start.11) | collective-permute-done | bytes 884768 | tf_op jit(solution)/shard_map/carried/ppermute | solution.py:433
  129.1 2.8 %add.1.refs_7_ = bf16[384,1152]{1,0:T(8,128)(2,1)} custom-call(f32[384,1152]{1,0:T(8,128)} %get-tuple-element.32.refs_0_, bf16[384,1152]{1,0:T(8,128)(2,1)} %copy-done.2, bf16[5,384,1152]{2,1,0:T(8,128)(2,1)} %bundle.1.refs_2_.refs_3_, bf16[384,1152]{1,0:T(8,128)(2,1)} %copy-done), custom_call_target="tpu_custom_call" | custom-call | flops 1 | tf_op jit(solution)/shard_map/add/pallas_call | solution.py:35
  131.9 3.0 %collective-permute-start.15 = (bf16[384,1152]{1,0:T(8,128)(2,1)}, bf16[384,1152]{1,0:T(8,128)(2,1)S(1)}, u32[]{:S(2)}, u32[]{:S(2)}) collective-permute-start(bf16[384,1152]{1,0:T(8,128)(2,1)} %add.1.refs_7_), channel_id=1, source_target_pairs={{0,2},{8,14},{2,4},{10,8},{4,6},{12,10},{6,0},{14,12},{1,3},{9,15}... | collective-permute-start | bytes 2654216 | tf_op jit(solution)/shard_map/late/ppermute | solution.py:433
  134.9 12.4 %cycle.1 = (f32[384,1152]{1,0:T(8,128)}, f32[384,1152]{1,0:T(8,128)}) custom-call(f32[2]{0:T(128)} %pad_maximum_fusion.refs_0_, bf16[400,1152]{1,0:T(8,128)(2,1)} %get-tuple-element.21.refs_1_.refs_3_, bf16[384,1152]{1,0:T(8,128)(2,1)} %get-tuple-element.22.refs_5_.refs_4_.refs_0_.refs_2_, bf16[5,384,1152]{2,1,0:T(8,128)(2,1)} %bundle.1.refs_2_.refs_3_, ...), custom_call_target="tpu_custom_call" | custom-call | flops 1 | tf_op jit(solution)/shard_map/cycle/pallas_call | solution.py:35
  148.3 1.3 collective-permute-start.13
  149.6 2.1 %collective-permute-done.13.refs_2_ = bf16[384,1152]{1,0:T(8,128)(2,1)S(1)} collective-permute-done((bf16[384,1152]{1,0:T(8,128)(2,1)}, bf16[384,1152]{1,0:T(8,128)(2,1)S(1)}, u32[]{:S(2)}, u32[]{:S(2)}) %collective-permute-start.13) | collective-permute-done | bytes 884768 | tf_op jit(solution)/shard_map/over_f1/ppermute | solution.py:529
  152.7 7.3 %last.1 = (f32[384,1152]{1,0:T(8,128)}, f32[384,1152]{1,0:T(8,128)}) custom-call(f32[2]{0:T(128)} %pad_maximum_fusion.refs_0_, bf16[384,1152]{1,0:T(8,128)(2,1)} %gate.5.refs_1_, bf16[384,1152]{1,0:T(8,128)(2,1)} %copy-done.10, bf16[400,1152]{1,0:T(8,128)(2,1)} %get-tuple-element.21.refs_1_.refs_3_, ...), custom_call_target="tpu_custom_call" | custom-call | flops 8000000000 | tf_op jit(solution)/shard_map/last/pallas_call | solution.py:35
  (42 shorter events, 10.7 us)
Async XLA Ops:
  5.4 20.6 %collective-permute-start.3 = (bf16[384,1152]{1,0:T(8,128)(2,1)}, bf16[384,1152]{1,0:T(8,128)(2,1)S(1)}, u32[]{:S(2)}, u32[]{:S(2)}) collective-permute-start(bf16[384,1152]{1,0:T(8,128)(2,1)} %get-tuple-element.23), channel_id=1, source_target_pairs={{0,16},{16,0},{32,48},{48,32},{1,17},{17,1},{33,49},{49,33},{2,18}... | collective-permute-start | bytes 2654216 | tf_op jit(solution)/shard_map/near/ppermute | solution.py:443
  5.5 23.6 %collective-permute-start.7 = (bf16[384,1152]{1,0:T(8,128)(2,1)}, bf16[384,1152]{1,0:T(8,128)(2,1)}, u32[]{:S(2)}, u32[]{:S(2)}) collective-permute-start(bf16[384,1152]{1,0:T(8,128)(2,1)} %get-tuple-element.22.refs_5_.refs_4_.refs_0_.refs_2_), channel_id=1, source_target_pairs={{0,2},{8,14},{2,4},{10,8},{4,6},{12,10},{6,0},{14,12},{1,3},{9,15}... | collective-permute-start | bytes 2654216 | tf_op jit(solution)/shard_map/one/ppermute | solution.py:433
  8.5 25.2 %collective-permute-start = (bf16[400,1152]{1,0:T(8,128)(2,1)}, bf16[400,1152]{1,0:T(8,128)(2,1)S(1)}, u32[]{:S(2)}, u32[]{:S(2)}) collective-permute-start(bf16[400,1152]{1,0:T(8,128)(2,1)} %get-tuple-element.21.refs_1_.refs_3_), channel_id=1, source_target_pairs={{0,1},{1,0},{2,3},{3,2},{4,5},{5,4},{6,7},{7,6},{8,9},{9,8},{10,11... | collective-permute-start | bytes 2764808 | tf_op jit(solution)/shard_map/other/ppermute | solution.py:28
  10.1 25.3 %collective-permute-start.8 = (bf16[384,1152]{1,0:T(8,128)(2,1)}, bf16[384,1152]{1,0:T(8,128)(2,1)}, u32[]{:S(2)}, u32[]{:S(2)}) collective-permute-start(bf16[384,1152]{1,0:T(8,128)(2,1)} %get-tuple-element.22.refs_5_.refs_4_.refs_0_.refs_2_), channel_id=1, source_target_pairs={{0,6},{8,10},{2,0},{10,12},{4,2},{12,14},{6,4},{14,8},{1,7},{9,11}... | collective-permute-start | bytes 2654216 | tf_op jit(solution)/shard_map/two/ppermute | solution.py:433
  10.1 45.8 %collective-permute-start.5 = (bf16[384,1152]{1,0:T(8,128)(2,1)}, bf16[384,1152]{1,0:T(8,128)(2,1)}, u32[]{:S(2)}, u32[]{:S(2)}) collective-permute-start(bf16[384,1152]{1,0:T(8,128)(2,1)} %get-tuple-element.25), channel_id=1, source_target_pairs={{16,32},{32,16},{17,33},{33,17},{18,34},{34,18},{19,35},{35,19},{2... | collective-permute-start | bytes 2654216 | tf_op jit(solution)/shard_map/mid/ppermute | solution.py:445
  26.9 56.5 %collective-permute-start.4 = (bf16[384,1152]{1,0:T(8,128)(2,1)}, bf16[384,1152]{1,0:T(8,128)(2,1)S(1)}, u32[]{:S(2)}, u32[]{:S(2)}) collective-permute-start(bf16[384,1152]{1,0:T(8,128)(2,1)} %gate.4), channel_id=1, source_target_pairs={{0,32},{32,0},{16,48},{48,16},{1,33},{33,1},{17,49},{49,17},{2,34}... | collective-permute-start | bytes 2654216 | tf_op jit(solution)/shard_map/far/ppermute | solution.py:447
  29.1 54.4 %collective-permute-start.9 = (bf16[384,1152]{1,0:T(8,128)(2,1)}, bf16[384,1152]{1,0:T(8,128)(2,1)}, u32[]{:S(2)}, u32[]{:S(2)}) collective-permute-start(bf16[384,1152]{1,0:T(8,128)(2,1)} %collective-permute-done.7.refs_3_.refs_2_), channel_id=1, source_target_pairs={{0,2},{8,14},{2,4},{10,8},{4,6},{12,10},{6,0},{14,12},{1,3},{9,15}... | collective-permute-start | bytes 2654216 | tf_op jit(solution)/shard_map/opp/ppermute | solution.py:433
  33.7 0.9 copy-start.1
  34.6 62.3 %collective-permute-start.1 = (bf16[384,1152]{1,0:T(8,128)(2,1)}, bf16[384,1152]{1,0:T(8,128)(2,1)S(1)}, u32[]{:S(2)}, u32[]{:S(2)}) collective-permute-start(bf16[384,1152]{1,0:T(8,128)(2,1)} %gate.3), channel_id=1, source_target_pairs={{48,64},{56,72},{0,240},{8,248},{112,128},{120,136},{64,48},{72,56... | collective-permute-start | bytes 2654216 | tf_op jit(solution)/shard_map/over_a/ppermute | solution.py:457
  35.4 61.6 %collective-permute-start.6 = (bf16[384,1152]{1,0:T(8,128)(2,1)}, bf16[384,1152]{1,0:T(8,128)(2,1)S(1)}, u32[]{:S(2)}, u32[]{:S(2)}) collective-permute-start(bf16[384,1152]{1,0:T(8,128)(2,1)} %gate.3), channel_id=1, source_target_pairs={{32,64},{40,72},{16,240},{24,248},{96,128},{104,136},{80,48},{88,5... | collective-permute-start | bytes 2654216 | tf_op jit(solution)/shard_map/over_b/ppermute | solution.py:457
  83.4 0.9 copy-start.6
  96.9 0.9 copy-start.5
  96.9 1.2 copy-start.9
  102.0 32.9 %collective-permute-start.10 = (bf16[5,384,1152]{2,1,0:T(8,128)(2,1)}, bf16[5,384,1152]{2,1,0:T(8,128)(2,1)}, u32[]{:S(2)}, u32[]{:S(2)}) collective-permute-start(bf16[5,384,1152]{2,1,0:T(8,128)(2,1)} %bundle.1.refs_2_.refs_3_), channel_id=1, source_target_pairs={{0,8},{8,0},{1,9},{9,1},{2,10},{10,2},{3,11},{11,3},{4,12},{12,4},... | collective-permute-start | bytes 13271048 | tf_op jit(solution)/shard_map/sib/ppermute | solution.py:28
  105.8 19.6 %collective-permute-start.12 = (bf16[384,1152]{1,0:T(8,128)(2,1)}, bf16[384,1152]{1,0:T(8,128)(2,1)S(1)}, u32[]{:S(2)}, u32[]{:S(2)}) collective-permute-start(bf16[384,1152]{1,0:T(8,128)(2,1)} %get-tuple-element.27.refs_4_), channel_id=1, source_target_pairs={{0,6},{8,10},{2,0},{10,12},{4,2},{12,14},{6,4},{14,8},{1,7},{9,11}... | collective-permute-start | bytes 2654216 | tf_op jit(solution)/shard_map/early/ppermute | solution.py:433
  107.1 21.1 %collective-permute-start.11 = (bf16[384,1152]{1,0:T(8,128)(2,1)}, bf16[384,1152]{1,0:T(8,128)(2,1)S(1)}, u32[]{:S(2)}, u32[]{:S(2)}) collective-permute-start(bf16[384,1152]{1,0:T(8,128)(2,1)} %get-tuple-element.33), channel_id=1, source_target_pairs={{0,2},{8,14},{2,4},{10,8},{4,6},{12,10},{6,0},{14,12},{1,3},{9,15}... | collective-permute-start | bytes 2654216 | tf_op jit(solution)/shard_map/carried/ppermute | solution.py:433
  108.5 38.8 %collective-permute-start.2 = (bf16[384,1152]{1,0:T(8,128)(2,1)}, bf16[384,1152]{1,0:T(8,128)(2,1)S(1)}, u32[]{:S(2)}, u32[]{:S(2)}) collective-permute-start(bf16[384,1152]{1,0:T(8,128)(2,1)} %copy-done.5), channel_id=1, source_target_pairs={{0,16},{48,32},{1,17},{49,33},{2,18},{50,34},{3,19},{51,35},{4,20}... | collective-permute-start | bytes 2654216 | tf_op jit(solution)/shard_map/over_f/ppermute | solution.py:516
  109.8 39.8 %collective-permute-start.14 = (bf16[384,1152]{1,0:T(8,128)(2,1)}, bf16[384,1152]{1,0:T(8,128)(2,1)S(1)}, u32[]{:S(2)}, u32[]{:S(2)}) collective-permute-start(bf16[384,1152]{1,0:T(8,128)(2,1)} %get-tuple-element.29.refs_7_), channel_id=1, source_target_pairs={{0,1},{1,0},{2,3},{3,2},{4,5},{5,4},{6,7},{7,6},{8,9},{9,8},{10,11... | collective-permute-start | bytes 2654216 | tf_op jit(solution)/shard_map/back/ppermute | solution.py:28
  125.3 2.9 %copy-start = (bf16[384,1152]{1,0:T(8,128)(2,1)}, bf16[384,1152]{1,0:T(8,128)(2,1)S(1)}, u32[]{:S(2)}) copy-start(bf16[384,1152]{1,0:T(8,128)(2,1)S(1)} %collective-permute-done.12.refs_3_.refs_8_.refs_10_) | copy-start | bytes 2654212
  131.9 17.7 %collective-permute-start.15 = (bf16[384,1152]{1,0:T(8,128)(2,1)}, bf16[384,1152]{1,0:T(8,128)(2,1)S(1)}, u32[]{:S(2)}, u32[]{:S(2)}) collective-permute-start(bf16[384,1152]{1,0:T(8,128)(2,1)} %add.1.refs_7_), channel_id=1, source_target_pairs={{0,2},{8,14},{2,4},{10,8},{4,6},{12,10},{6,0},{14,12},{1,3},{9,15}... | collective-permute-start | bytes 2654216 | tf_op jit(solution)/shard_map/late/ppermute | solution.py:433
  148.3 3.5 %collective-permute-start.13 = (bf16[384,1152]{1,0:T(8,128)(2,1)}, bf16[384,1152]{1,0:T(8,128)(2,1)S(1)}, u32[]{:S(2)}, u32[]{:S(2)}) collective-permute-start(bf16[384,1152]{1,0:T(8,128)(2,1)} %gate.5.refs_1_), channel_id=1, source_target_pairs={{24,16},{32,40},{25,17},{33,41},{26,18},{34,42},{27,19},{35,43},{2... | collective-permute-start | bytes 2654216 | tf_op jit(solution)/shard_map/over_f1/ppermute | solution.py:529
  149.6 2.2 %copy-start.7 = (bf16[384,1152]{1,0:T(8,128)(2,1)}, bf16[384,1152]{1,0:T(8,128)(2,1)S(1)}, u32[]{:S(2)}) copy-start(bf16[384,1152]{1,0:T(8,128)(2,1)S(1)} %collective-permute-done.14.refs_7_) | copy-start | bytes 2654212
  149.6 2.2 %copy-start.8 = (bf16[384,1152]{1,0:T(8,128)(2,1)}, bf16[384,1152]{1,0:T(8,128)(2,1)S(1)}, u32[]{:S(2)}) copy-start(bf16[384,1152]{1,0:T(8,128)(2,1)S(1)} %collective-permute-done.15.refs_11_) | copy-start | bytes 2654212
  151.8 0.9 copy-start.10
  (3 other events, 2.7 us)

commit v2 on v0

--- a/solution.py
+++ b/solution.py
@@ -15,7 +15,6 @@
 F32 = jnp.float32
 SM = pl.BlockSpec(memory_space=pltpu.SMEM)
 ANY = pl.BlockSpec(memory_space=pltpu.HBM)
-FREE = pl.BlockSpec(memory_space=pl.ANY)
 WHOLE, WHOLE32 = ((ROWS, WIDTH), BF16), ((ROWS, WIDTH), F32)
 
 
@@ -28,18 +27,18 @@
     return lax.ppermute(x, axis, [(i, (i + by) % size) for i in range(size)])
 
 
-def call(body, outs, args, scratch, name, smem=0, space=ANY, limit=60, flops=8_000_000_000):
+def call(body, outs, args, scratch, name, smem=0):
     def kernel(*refs):
         body(Copies(refs[-1]), *refs[:-1])
 
     return pl.pallas_call(
         kernel,
         out_shape=[jax.ShapeDtypeStruct(s, d) for s, d in outs],
-        in_specs=[SM] * smem + [space] * (len(args) - smem),
+        in_specs=[SM] * smem + [ANY] * (len(args) - smem),
         out_specs=[ANY] * len(outs),
         scratch_shapes=list(scratch) + [pltpu.SemaphoreType.DMA((32,))],
-        cost_estimate=pl.CostEstimate(flops=flops, bytes_accessed=0, transcendentals=0),
-        compiler_params=pltpu.CompilerParams(vmem_limit_bytes=limit * 2**20),
+        cost_estimate=pl.CostEstimate(flops=20_000_000_000, bytes_accessed=0, transcendentals=0),
+        compiler_params=pltpu.CompilerParams(vmem_limit_bytes=60 * 2**20),
         name=name,
     )(*args)
 
@@ -83,10 +82,10 @@
 
 
 def unit_kernel(
-    copies, ids_ref, cap_ref, pic_ref, text_out, image_out, wrap_out, even_out, low_out,
-    cap, pic, text, image, wrap, even, low,
-):
-    x = lax.axis_index("x")
+    copies, ids_ref, cap_ref, pic_ref, text_out, image_out, wrap_out, turn_out,
+    cap, pic, text, image, wrap, turns,
+):
+    x, core = lax.axis_index("x"), lax.axis_index("c")
     come = [
         [copies.go(src.at[pl.ds(k * HALF, HALF)], dst.at[pl.ds(k * HALF, HALF)])
          for src, dst in ((cap_ref, cap), (pic_ref, pic))]
@@ -112,10 +111,13 @@
         i = (v * inverse_length(v)).astype(BF16)
         image[at, :] = i
         wrap[at, :] = jnp.where(x >= 2, t, i)
-        even[at, :] = jnp.where(lax.rem(x, 2) == 0, t, i)
-        low[at, :] = jnp.where(x < 2, t, i)
-        for src, dst in ((text, text_out), (wrap, wrap_out), (even, even_out), (low, low_out)):
+        for j in range(4):
+            ahead = jnp.logical_or(x < j, jnp.logical_and(x == j, core == 0))
+            turns[j, at, :] = jnp.where(ahead, t, i)
+        for src, dst in ((text, text_out), (wrap, wrap_out)):
             leave.append(copies.go(src.at[at], dst.at[at]))
+        for j in range(4):
+            leave.append(copies.go(turns.at[j, at], turn_out.at[j, at]))
         if k == 0:
             leave.append(copies.go(image.at[at], image_out.at[at]))
         else:
@@ -196,7 +198,7 @@
 
 
 def opposite_kernel(
-    copies, par_ref, image_ref, other_ref, opp_ref, after_ref, then_ref, return_out, wt_out,
+    copies, par_ref, image_ref, other_ref, opp_ref, after_ref, return_out, wt_out,
     x_scr, near, far, text, back, wt,
 ):
     images = fetch_images(copies, image_ref, other_ref, x_scr, near, far)
@@ -212,8 +214,8 @@
 
 
 def image_kernel(
-    copies, wt3_ref, wt_ref, one_ref, two_ref, text_ref, opp_ref, image_ref, from_one,
-    from_two, from_three, aw, bw, far_out, near_out, own_out, w_scr, t_scr, far, near,
+    copies, wt3_ref, wt_ref, one_ref, two_ref, text_ref, opp_ref, far_out, near_out,
+    w_scr, t_scr, far, near,
 ):
     come = [
         copies.go(wt3_ref, w_scr.at[pl.ds(0, 3 * ROWS)]),
@@ -221,18 +223,10 @@
     ]
     for k, ref in enumerate((one_ref, two_ref, text_ref, opp_ref)):
         come.append(copies.go(ref, t_scr.at[pl.ds(k * ROWS, ROWS)]))
-    image = image_ref.at[pl.ds(0, ROWS)]
-    leave = [copies.pick(lax.axis_index("c") == 0, text_ref, image, own_out.at[0])]
-    x = lax.axis_index("x")
-    inner = jnp.logical_or(x == 1, x == 2)
-    for k, ref in enumerate((from_one, from_two)):
-        leave.append(copies.go(ref, own_out.at[k + 1]))
-    leave.append(copies.pick(inner, from_three, aw, own_out.at[3]))
-    leave.append(copies.go(bw, own_out.at[4]))
     for copy in come:
         copy.wait()
     far[...] = tn(w_scr[:, ROWS:], t_scr[...]).astype(BF16)
-    leave.append(copies.go(far, far_out))
+    leave = [copies.go(far, far_out)]
     near[...] = tn(w_scr[:, :ROWS], t_scr[...])
     leave.append(copies.go(near, near_out))
     for copy in leave:
@@ -247,7 +241,7 @@
 
 
 def cycle_kernel(
-    copies, par_ref, image_ref, text_ref, own, sib, gi_ref, gt_ref,
+    copies, par_ref, image_ref, text_ref, own, sib, aw, sa, bw, sb, gi_ref, gt_ref,
     after_ref, early_ref, gi_out, gt_out, image, text, gi, gt, t_scr, i_scr, w_scr,
 ):
     x, core = lax.axis_index("x"), lax.axis_index("c")
@@ -258,20 +252,22 @@
     ):
         d = x if low else 3 - x
         e = core if low else 1 - core
+        at = lambda ref, i: ref.at[jnp.clip(i if low else 3 - i, 0, 3)]
         slot = lambda k: scr.at[pl.ds(k * ROWS, ROWS)]
-
-        def place(i, beyond):
-            inside = jnp.bitwise_xor(x, jnp.clip(i if low else 3 - i, 0, 3))
-            return jnp.where(i >= 0, inside, beyond)
-
-        swapped = jnp.logical_and(d == 0, e == 1)
+        last = d - 2 + e
         here = [
             copies.go(mine_ref.at[pl.ds(0, ROWS)], mine),
-            copies.go(own.at[place(d - 1, 3)], slot(0)),
-            copies.go(own.at[place(d - 2, 4)], slot(1)),
-            copies.go(sib.at[place(d - 1 + e, 3)], slot(2)),
-            copies.go(sib.at[place(d - 2 + e, jnp.where(swapped, 3, 4))], slot(3)),
+            copies.pick(d >= 1, at(own, d - 1), aw, slot(0)),
+            copies.pick(d >= 2, at(own, d - 2), bw, slot(1)),
+            copies.pick(d - 1 + e >= 0, at(sib, d - 1 + e), sa, slot(2)),
         ]
+        copy = copies.of(sb, slot(3))
+        sem = copies.sems.at[copies.count - 1]
+        pl.when(last >= 0)(pltpu.make_async_copy(at(sib, last), slot(3), sem).start)
+        swapped = jnp.logical_and(d == 0, e == 1)
+        pl.when(swapped)(pltpu.make_async_copy(sa, slot(3), sem).start)
+        pl.when(jnp.logical_and(last < 0, jnp.logical_not(swapped)))(copy.start)
+        here.append(copy)
         here.append(copies.go(grad_ref, grad))
         come.append(here)
     leave = []
@@ -287,7 +283,7 @@
         copy.wait()
 
 
-def add_kernel(copies, late_ref, return_ref, after_ref, then_ref, out_ref, late, back, out):
+def add_kernel(copies, late_ref, return_ref, after_ref, out_ref, late, back, out):
     come = [copies.go(late_ref, late), copies.go(return_ref, back)]
     for copy in come:
         copy.wait()
@@ -353,10 +349,10 @@
     return pl.pallas_call(
         gate_kernel,
         out_shape=jax.ShapeDtypeStruct(block.shape, block.dtype),
-        in_specs=[FREE, FREE],
-        out_specs=FREE,
+        in_specs=[ANY, ANY],
+        out_specs=ANY,
         input_output_aliases={0: 0},
-        compiler_params=pltpu.CompilerParams(vmem_limit_bytes=2**20),
+        compiler_params=pltpu.CompilerParams(vmem_limit_bytes=60 * 2**20),
         name="gate",
     )(block, after)
 
@@ -365,11 +361,11 @@
     pics, caps = pictures[0, 0], captions[0, 0]
     par = jnp.stack([sharpness, offset])
     counts = [vm(16), vm(16)]
-    text, image, wrap, even, low = call(
+    text, image, wrap, turns = call(
         unit_kernel,
-        [WHOLE, ((ROWS + 16, WIDTH), BF16), WHOLE, WHOLE, WHOLE],
+        [WHOLE, ((ROWS + 16, WIDTH), BF16), WHOLE, ((4, ROWS, WIDTH), BF16)],
         (tile_numbers[0, 0].T, caps, pics),
-        [vm(ROWS), vm(ROWS), vm(ROWS), vm(ROWS + 16), vm(ROWS), vm(ROWS), vm(ROWS)],
+        [vm(ROWS), vm(ROWS), vm(ROWS), vm(ROWS + 16), vm(ROWS), pltpu.VMEM((4, ROWS, WIDTH), BF16)],
         "unit",
         1,
     )
@@ -394,12 +390,8 @@
             [(turn(x, 0), turn(x, 0)) for x in range(4)]
             + [(turn(a, 1), turn(b, 1)) for a, b in ((3, 0), (2, 1), (1, 2), (0, 3))],
         )
-    with jax.named_scope("near"):
-        from_one = lax.ppermute(even, "x", [(0, 1), (1, 0), (2, 3), (3, 2)])
-    with jax.named_scope("mid"):
-        from_three = lax.ppermute(low, "x", [(1, 2), (2, 1)])
-    with jax.named_scope("far"):
-        from_two = lax.ppermute(gate(low, from_one), "x", [(0, 2), (2, 0), (1, 3), (3, 1)])
+    with jax.named_scope("turns"):
+        own = lax.all_to_all(turns, "x", split_axis=0, concat_axis=0, tiled=True)
     with jax.named_scope("opp"):
         text_opp = along_y(text_one, 1)
     hop = gate(hop, other)
@@ -430,18 +422,20 @@
     part_opp, wt = call(
         opposite_kernel,
         [WHOLE, ((ROWS, 2 * ROWS), BF16)],
-        (par, image, other, text_opp, part_early, from_three),
+        (par, image, other, text_opp, part_early),
         [vm(2 * ROWS), *counts, vm(ROWS), vm(ROWS), vm(ROWS, 2 * ROWS)],
         "opposite",
         1,
     )
     with jax.named_scope("carried"):
         carried = along_y(part_opp, 1)
-    grad_far, grad_image, own = call(
+    own = gate(own, part_opp)
+    with jax.named_scope("sib"):
+        sib = ring(own, "c", 1)
+    grad_far, grad_image = call(
         image_kernel,
-        [WHOLE, WHOLE32, ((5, ROWS, WIDTH), BF16)],
-        (wt3, wt, text_one, text_two, text, text_opp, image, from_one, from_two, from_three,
-         over_a, over_b),
+        [WHOLE, WHOLE32],
+        (wt3, wt, text_one, text_two, text, text_opp),
         [vm(4 * ROWS, 2 * ROWS), vm(4 * ROWS), vm(ROWS), vm(ROWS, dtype=F32)],
         "image_side",
     )
@@ -450,28 +444,30 @@
     part_late = call(
         add_kernel,
         [WHOLE],
-        (part_late, carried, grad_far, early),
+        (part_late, carried, grad_far),
         [vm(ROWS, dtype=F32), vm(ROWS), vm(ROWS)],
         "add",
-        flops=1,
     )[0]
     with jax.named_scope("late"):
         late = along_y(part_late, 1)
 
-    with jax.named_scope("sib"):
-        sib = ring(gate(own, part_late), "c", 1)
-
     with jax.named_scope("over_f"):
         over_f = lax.ppermute(over_a, "x", [(0, 1), (3, 2)])
+    with jax.named_scope("over_a1"):
+        over_a1 = ring(over_a, "c", 1)
+    with jax.named_scope("over_b1"):
+        over_b1 = lax.ppermute(
+            over_b, ("x", "c"), [(turn(0, 1), turn(0, 0)), (turn(3, 0), turn(3, 1))]
+        )
     grad_image, grad_text = call(
         cycle_kernel,
         [WHOLE32, WHOLE32],
-        (par, image, text, own, sib, grad_image, grad_text, part_late, early),
+        (par, image, text, own, sib, over_a, over_a1, over_b, over_b1, grad_image, grad_text,
+         part_late, early),
         [vm(ROWS), vm(ROWS), vm(ROWS, dtype=F32), vm(ROWS, dtype=F32), vm(4 * ROWS),
          vm(4 * ROWS), vm(ROWS, 4 * ROWS)],
         "cycle",
         1,
-        flops=1,
     )
     over_f = gate(over_f, grad_image)
     with jax.named_scope("over_f1"):
@@ -487,8 +483,6 @@
          vm(ROWS, dtype=F32), vm(ROWS), vm(ROWS), vm(ROWS, dtype=F32), vm(ROWS), vm(ROWS)],
         "last",
         1,
-        FREE,
-        24,
     )
     return (image_grad[None, None], text_grad[None, None])
 

time: 277 us -> 134 us (0.48)
  Pallas kernels: 178 us -> 50.9 us
  waiting for transfers between devices: 52.3 us -> 30.8 us
  starting transfers between devices: 24.8 us -> 44.1 us
  local copies, waits for them, and re-layouts: 18.3 us -> 3.71 us
    pallas_call x7, Pallas kernels: 178 us -> 50.9 us  [call(): pl.pallas_call(kernel, out_shape=[jax.ShapeDtypeStruct(s, d) for s, d in...]
    ppermute x1, waiting for transfers between devices: 23 us -> 0.97 us  [local(): lax.ppermute(wrap, ('x', 'c'), [(turn(x, 0), turn(x, 0)) for x in range(4...]
    unnamed x41 -> x12, local copies, waits for them, and re-layouts: 18.3 us -> 3.71 us
    ppermute x3 -> x1, waiting for transfers between devices: 13.3 us -> 0.01 us  [local(): lax.ppermute(over_b, ('x', 'c'), [(turn(0, 1), turn(0, 0)), (turn(3, 0),...]
    all_to_all x0 -> x1, waiting for transfers between devices: none -> 13.3 us  [local(): own = lax.all_to_all(turns, 'x', split_axis=0, concat_axis=0, tiled=True)]
    ppermute x2, starting transfers between devices: 2.95 us -> 11.5 us  [over(): return lax.ppermute(hop, GROUP, sends)]
    ppermute x1, waiting for transfers between devices: 5.21 us -> 11.1 us  [local(): over_f = lax.ppermute(over_a, 'x', [(0, 1), (3, 2)])]
    all_to_all x0 -> x1, starting transfers between devices: none -> 5.23 us  [local(): own = lax.all_to_all(turns, 'x', split_axis=0, concat_axis=0, tiled=True)]
  transfers between devices with their start and end apart: 17 -> 17, of which waited for: 7 -> 5; matrix products, arithmetic and copies ran while one was open for 2% -> 0% of each run, Pallas kernels for 59% -> 29%
where the time goes in v2:
time: 134 us; the launch traced here: 132 us
  Pallas kernels  50.9 us (38%)
  starting transfers between devices  44.1 us (33%)
  waiting for transfers between devices  30.8 us (23%)
  local copies, waits for them, and re-layouts  3.71 us (3%)
  between operations  2.27 us (2%)
    pallas_call x7, Pallas kernels, call(): pl.pallas_call(kernel, out_shape=[jax.ShapeDtypeStruct(s, d) for s, d in...  50.9 us
    all_to_all x1, waiting for transfers between devices, local(): own = lax.all_to_all(turns, 'x', split_axis=0, concat_axis=0, tiled=True)  13.3 us
    ppermute x2, starting transfers between devices, over(): return lax.ppermute(hop, GROUP, sends)  11.5 us
    ppermute x6, starting transfers between devices, along_y(): return lax.ppermute(block, ('c', 'y'), pairs)  11.3 us
    ppermute x1, waiting for transfers between devices, local(): over_f = lax.ppermute(over_a, 'x', [(0, 1), (3, 2)])  11.1 us
    ppermute x4, starting transfers between devices, ring(): return lax.ppermute(x, axis, [(i, (i + by) % size) for i in range(size)])  8.72 us
    all_to_all x1, starting transfers between devices, local(): own = lax.all_to_all(turns, 'x', split_axis=0, concat_axis=0, tiled=True)  5.23 us
    unnamed x12, local copies, waits for them, and re-layouts  3.71 us
  transfers between devices with their start and end apart: 17, of which 5 were waited for; matrix products, arithmetic and copies ran while one was open for 0% of the time, Pallas kernels for 29%

profile of v2, /device:TPU:3, one launch (start us, length us, event | category | flops | bytes accessed | tf_op | source)
XLA Modules:
  0.0 132.4 jit_solution(10058368583040013802)
XLA Ops:
  0.6 5.0 %unit.1 = (bf16[384,1152]{1,0:T(8,128)(2,1)}, bf16[400,1152]{1,0:T(8,128)(2,1)}, bf16[384,1152]{1,0:T(8,128)(2,1)}, bf16[4,384,1152]{2,1,0:T(8,128)(2,1)}) custom-call(s32[2,8]{1,0:T(2,128)} %bitcast.15, bf16[384,1152]{1,0:T(8,128)(2,1)} %bitcast.11, bf16[384,1152]{1,0:T(8,128)(2,1)} %bitcast.13), custom_call_target="tpu_custom_call" | custom-call | flops 20000000000 | tf_op jit(solution)/shard_map/unit/pallas_call | solution.py:34
  5.7 1.7 %collective-permute-start.1 = (bf16[400,1152]{1,0:T(8,128)(2,1)}, bf16[400,1152]{1,0:T(8,128)(2,1)}, u32[]{:S(2)}, u32[]{:S(2)}) collective-permute-start(bf16[400,1152]{1,0:T(8,128)(2,1)} %get-tuple-element.19.refs_1_.refs_3_), channel_id=1, source_target_pairs={{0,1},{1,0},{2,3},{3,2},{4,5},{5,4},{6,7},{7,6},{8,9},{9,8},{10,11... | collective-permute-start | bytes 2764808 | tf_op jit(solution)/shard_map/other/ppermute | solution.py:27
  7.4 2.7 %collective-permute-start.4 = (bf16[384,1152]{1,0:T(8,128)(2,1)}, bf16[384,1152]{1,0:T(8,128)(2,1)}, u32[]{:S(2)}, u32[]{:S(2)}) collective-permute-start(bf16[384,1152]{1,0:T(8,128)(2,1)} %get-tuple-element.20.refs_5_.refs_4_.refs_2_), channel_id=1, source_target_pairs={{0,2},{8,14},{2,4},{10,8},{4,6},{12,10},{6,0},{14,12},{1,3},{9,15}... | collective-permute-start | bytes 2654216 | tf_op jit(solution)/shard_map/one/ppermute | solution.py:377
  10.1 3.1 %collective-permute-start = (bf16[384,1152]{1,0:T(8,128)(2,1)}, bf16[384,1152]{1,0:T(8,128)(2,1)}, u32[]{:S(2)}, u32[]{:S(2)}) collective-permute-start(bf16[384,1152]{1,0:T(8,128)(2,1)} %get-tuple-element.18), channel_id=1, source_target_pairs={{0,0},{16,16},{32,32},{48,48},{56,8},{40,24},{24,40},{8,56},{1,1},... | collective-permute-start | bytes 2654216 | tf_op jit(solution)/shard_map/hop/ppermute | solution.py:387
  13.3 5.2 %all-to-all-start = ((bf16[4,384,1152]{2,1,0:T(8,128)(2,1)}), bf16[4,384,1152]{2,1,0:T(8,128)(2,1)S(1)}, u32[]{:S(2)}, u32[]{:S(2)}) async-start(bf16[4,384,1152]{2,1,0:T(8,128)(2,1)} %get-tuple-element.21), calls=%async_computation | async-start | bytes 7077888 | tf_op jit(solution)/shard_map/turns/all_to_all | solution.py:394
  20.5 3.1 %collective-permute-start.5 = (bf16[384,1152]{1,0:T(8,128)(2,1)}, bf16[384,1152]{1,0:T(8,128)(2,1)}, u32[]{:S(2)}, u32[]{:S(2)}) collective-permute-start(bf16[384,1152]{1,0:T(8,128)(2,1)} %collective-permute-done.4.refs_3_.refs_2_), channel_id=1, source_target_pairs={{0,2},{8,14},{2,4},{10,8},{4,6},{12,10},{6,0},{14,12},{1,3},{9,15}... | collective-permute-start | bytes 2654216 | tf_op jit(solution)/shard_map/opp/ppermute | solution.py:377
  24.5 3.2 %collective-permute-done.1.after_ref.refs_2_ = bf16[400,1152]{1,0:T(8,128)(2,1)} collective-permute-done((bf16[400,1152]{1,0:T(8,128)(2,1)}, bf16[400,1152]{1,0:T(8,128)(2,1)}, u32[]{:S(2)}, u32[]{:S(2)}) %collective-permute-start.1) | collective-permute-done | bytes 921632 | tf_op jit(solution)/shard_map/other/ppermute | solution.py:27
  27.8 1.6 %collective-permute-start.2 = (bf16[384,1152]{1,0:T(8,128)(2,1)}, bf16[384,1152]{1,0:T(8,128)(2,1)}, u32[]{:S(2)}, u32[]{:S(2)}) collective-permute-start(bf16[384,1152]{1,0:T(8,128)(2,1)} %gate.3.refs_6_), channel_id=1, source_target_pairs={{48,64},{0,240},{8,72},{56,248},{112,128},{64,48},{72,136},{120,56... | collective-permute-start | bytes 2654216 | tf_op jit(solution)/shard_map/over_a/ppermute | solution.py:404
  29.4 9.9 %collective-permute-start.9 = (bf16[384,1152]{1,0:T(8,128)(2,1)}, bf16[384,1152]{1,0:T(8,128)(2,1)}, u32[]{:S(2)}, u32[]{:S(2)}) collective-permute-start(bf16[384,1152]{1,0:T(8,128)(2,1)} %gate.3.refs_6_), channel_id=1, source_target_pairs={{32,64},{16,240},{24,72},{40,248},{96,128},{80,48},{88,136},{104,5... | collective-permute-start | bytes 2654216 | tf_op jit(solution)/shard_map/over_b/ppermute | solution.py:404
  39.3 10.6 %hard.1 = (bf16[384,1152]{1,0:T(8,128)(2,1)}, f32[384,1152]{1,0:T(8,128)}, f32[384,1152]{1,0:T(8,128)}, bf16[1152,768]{1,0:T(8,128)(2,1)}) custom-call(f32[2]{0:T(128)} %pad_maximum_fusion.refs_0_, bf16[400,1152]{1,0:T(8,128)(2,1)} %get-tuple-element.19.refs_1_.refs_3_, bf16[400,1152]{1,0:T(8,128)(2,1)} %collective-permute-done.1.after_ref.refs_2_, ...), custom_call_target="tpu_custom_call" | custom-call | flops 20000000000 | tf_op jit(solution)/shard_map/hard/pallas_call | solution.py:34
  49.9 1.4 %collective-permute-start.12 = (bf16[384,1152]{1,0:T(8,128)(2,1)}, bf16[384,1152]{1,0:T(8,128)(2,1)}, u32[]{:S(2)}, u32[]{:S(2)}) collective-permute-start(bf16[384,1152]{1,0:T(8,128)(2,1)} %get-tuple-element.22.refs_4_), channel_id=1, source_target_pairs={{0,6},{8,10},{2,0},{10,12},{4,2},{12,14},{6,4},{14,8},{1,7},{9,11}... | collective-permute-start | bytes 2654216 | tf_op jit(solution)/shard_map/early/ppermute | solution.py:377
  51.3 5.5 %opposite.1 = (bf16[384,1152]{1,0:T(8,128)(2,1)}, bf16[384,768]{1,0:T(8,128)(2,1)}) custom-call(f32[2]{0:T(128)} %pad_maximum_fusion.refs_0_, bf16[400,1152]{1,0:T(8,128)(2,1)} %get-tuple-element.19.refs_1_.refs_3_, bf16[400,1152]{1,0:T(8,128)(2,1)} %collective-permute-done.1.after_ref.refs_2_, bf16[384,1152]{1,0:T(8,128)(2,1)} %collective-permute-done.5.refs_3_.refs_5_, ...), custom_call_target="tpu_custom_call" | custom-call | flops 20000000000 | tf_op jit(solution)/shard_map/opposite/pallas_call | solution.py:34
  56.8 1.5 %collective-permute-start.11 = (bf16[384,1152]{1,0:T(8,128)(2,1)}, bf16[384,1152]{1,0:T(8,128)(2,1)}, u32[]{:S(2)}, u32[]{:S(2)}) collective-permute-start(bf16[384,1152]{1,0:T(8,128)(2,1)} %get-tuple-element.23.after_ref), channel_id=1, source_target_pairs={{0,2},{8,14},{2,4},{10,8},{4,6},{12,10},{6,0},{14,12},{1,3},{9,15}... | collective-permute-start | bytes 2654216 | tf_op jit(solution)/shard_map/carried/ppermute | solution.py:377
  58.3 13.3 %all-to-all-done.block_ref = bf16[4,384,1152]{2,1,0:T(8,128)(2,1)S(1)} async-done(((bf16[4,384,1152]{2,1,0:T(8,128)(2,1)}), bf16[4,384,1152]{2,1,0:T(8,128)(2,1)S(1)}, u32[]{:S(2)}, u32[]{:S(2)}) %all-to-all-start) | async-done | bytes 3538976 | tf_op jit(solution)/shard_map/turns/all_to_all | solution.py:394
  71.6 1.8 %copy-done = bf16[4,384,1152]{2,1,0:T(8,128)(2,1)} copy-done((bf16[4,384,1152]{2,1,0:T(8,128)(2,1)}, bf16[4,384,1152]{2,1,0:T(8,128)(2,1)S(1)}, u32[]{:S(2)}) %copy-start) | copy-done | bytes 3538968
  73.4 6.7 %collective-permute-start.7 = (bf16[4,384,1152]{2,1,0:T(8,128)(2,1)}, bf16[4,384,1152]{2,1,0:T(8,128)(2,1)}, u32[]{:S(2)}, u32[]{:S(2)}) collective-permute-start(bf16[4,384,1152]{2,1,0:T(8,128)(2,1)} %gate.4.refs_3_), channel_id=1, source_target_pairs={{0,8},{8,0},{1,9},{9,1},{2,10},{10,2},{3,11},{11,3},{4,12},{12,4},... | collective-permute-start | bytes 10616840 | tf_op jit(solution)/shard_map/sib/ppermute | solution.py:27
  80.1 7.4 %image_side.1 = (bf16[384,1152]{1,0:T(8,128)(2,1)}, f32[384,1152]{1,0:T(8,128)}) custom-call(bf16[1152,768]{1,0:T(8,128)(2,1)} %get-tuple-element.24.refs_0_, bf16[384,768]{1,0:T(8,128)(2,1)} %get-tuple-element.25.refs_1_, bf16[384,1152]{1,0:T(8,128)(2,1)} %collective-permute-done.4.refs_3_.refs_2_, ...), custom_call_target="tpu_custom_call" | custom-call | flops 20000000000 | tf_op jit(solution)/shard_map/image_side/pallas_call | solution.py:34
  87.9 1.6 %collective-permute-start.10 = (bf16[384,1152]{1,0:T(8,128)(2,1)}, bf16[384,1152]{1,0:T(8,128)(2,1)}, u32[]{:S(2)}, u32[]{:S(2)}) collective-permute-start(bf16[384,1152]{1,0:T(8,128)(2,1)} %collective-permute-done.9.refs_7_), channel_id=1, source_target_pairs={{8,0},{48,56},{9,1},{49,57},{10,2},{50,58},{11,3},{51,59},{12,4},{... | collective-permute-start | bytes 2654216 | tf_op jit(solution)/shard_map/over_b1/ppermute | solution.py:459
  89.4 3.1 %add.1.refs_11_ = bf16[384,1152]{1,0:T(8,128)(2,1)} custom-call(f32[384,1152]{1,0:T(8,128)} %get-tuple-element.28.refs_0_, bf16[384,1152]{1,0:T(8,128)(2,1)} %collective-permute-done.11.refs_1_, bf16[384,1152]{1,0:T(8,128)(2,1)} %get-tuple-element.29.refs_2_), custom_call_target="tpu_custom_call" | custom-call | flops 20000000000 | tf_op jit(solution)/shard_map/add/pallas_call | solution.py:34
  93.8 2.6 %collective-permute-start.15 = (bf16[384,1152]{1,0:T(8,128)(2,1)}, bf16[384,1152]{1,0:T(8,128)(2,1)S(1)}, u32[]{:S(2)}, u32[]{:S(2)}) collective-permute-start(bf16[384,1152]{1,0:T(8,128)(2,1)} %add.1.refs_11_), channel_id=1, source_target_pairs={{0,2},{8,14},{2,4},{10,8},{4,6},{12,10},{6,0},{14,12},{1,3},{9,15}... | collective-permute-start | bytes 2654216 | tf_op jit(solution)/shard_map/late/ppermute | solution.py:377
  96.4 11.5 %cycle.1 = (f32[384,1152]{1,0:T(8,128)}, f32[384,1152]{1,0:T(8,128)}) custom-call(f32[2]{0:T(128)} %pad_maximum_fusion.refs_0_, bf16[400,1152]{1,0:T(8,128)(2,1)} %get-tuple-element.19.refs_1_.refs_3_, bf16[384,1152]{1,0:T(8,128)(2,1)} %get-tuple-element.20.refs_5_.refs_4_.refs_2_, bf16[4,384,1152]{2,1,0:T(8,128)(2,1)} %gate.4.refs_3_, ...), custom_call_target="tpu_custom_call" | custom-call | flops 20000000000 | tf_op jit(solution)/shard_map/cycle/pallas_call | solution.py:34
  107.9 11.1 %collective-permute-done.3.block_ref = bf16[384,1152]{1,0:T(8,128)(2,1)S(1)} collective-permute-done((bf16[384,1152]{1,0:T(8,128)(2,1)}, bf16[384,1152]{1,0:T(8,128)(2,1)S(1)}, u32[]{:S(2)}, u32[]{:S(2)}) %collective-permute-start.3) | collective-permute-done | bytes 884768 | tf_op jit(solution)/shard_map/over_f/ppermute | solution.py:455
  121.4 2.1 %collective-permute-done.13.refs_2_ = bf16[384,1152]{1,0:T(8,128)(2,1)S(1)} collective-permute-done((bf16[384,1152]{1,0:T(8,128)(2,1)}, bf16[384,1152]{1,0:T(8,128)(2,1)S(1)}, u32[]{:S(2)}, u32[]{:S(2)}) %collective-permute-start.13) | collective-permute-done | bytes 884768 | tf_op jit(solution)/shard_map/over_f1/ppermute | solution.py:474
  124.5 7.7 %last.1 = (f32[384,1152]{1,0:T(8,128)}, f32[384,1152]{1,0:T(8,128)}) custom-call(f32[2]{0:T(128)} %pad_maximum_fusion.refs_0_, bf16[384,1152]{1,0:T(8,128)(2,1)} %gate.5.refs_1_, bf16[384,1152]{1,0:T(8,128)(2,1)} %copy-done.5, bf16[400,1152]{1,0:T(8,128)(2,1)} %get-tuple-element.19.refs_1_.refs_3_, ...), custom_call_target="tpu_custom_call" | custom-call | flops 20000000000 | tf_op jit(solution)/shard_map/last/pallas_call | solution.py:34
  (33 shorter events, 6.5 us)
Async XLA Ops:
  5.7 22.1 %collective-permute-start.1 = (bf16[400,1152]{1,0:T(8,128)(2,1)}, bf16[400,1152]{1,0:T(8,128)(2,1)}, u32[]{:S(2)}, u32[]{:S(2)}) collective-permute-start(bf16[400,1152]{1,0:T(8,128)(2,1)} %get-tuple-element.19.refs_1_.refs_3_), channel_id=1, source_target_pairs={{0,1},{1,0},{2,3},{3,2},{4,5},{5,4},{6,7},{7,6},{8,9},{9,8},{10,11... | collective-permute-start | bytes 2764808 | tf_op jit(solution)/shard_map/other/ppermute | solution.py:27
  7.4 13.1 %collective-permute-start.4 = (bf16[384,1152]{1,0:T(8,128)(2,1)}, bf16[384,1152]{1,0:T(8,128)(2,1)}, u32[]{:S(2)}, u32[]{:S(2)}) collective-permute-start(bf16[384,1152]{1,0:T(8,128)(2,1)} %get-tuple-element.20.refs_5_.refs_4_.refs_2_), channel_id=1, source_target_pairs={{0,2},{8,14},{2,4},{10,8},{4,6},{12,10},{6,0},{14,12},{1,3},{9,15}... | collective-permute-start | bytes 2654216 | tf_op jit(solution)/shard_map/one/ppermute | solution.py:377
  10.1 14.4 %collective-permute-start = (bf16[384,1152]{1,0:T(8,128)(2,1)}, bf16[384,1152]{1,0:T(8,128)(2,1)}, u32[]{:S(2)}, u32[]{:S(2)}) collective-permute-start(bf16[384,1152]{1,0:T(8,128)(2,1)} %get-tuple-element.18), channel_id=1, source_target_pairs={{0,0},{16,16},{32,32},{48,48},{56,8},{40,24},{24,40},{8,56},{1,1},... | collective-permute-start | bytes 2654216 | tf_op jit(solution)/shard_map/hop/ppermute | solution.py:387
  13.2 26.0 %collective-permute-start.6 = (bf16[384,1152]{1,0:T(8,128)(2,1)}, bf16[384,1152]{1,0:T(8,128)(2,1)}, u32[]{:S(2)}, u32[]{:S(2)}) collective-permute-start(bf16[384,1152]{1,0:T(8,128)(2,1)} %get-tuple-element.20.refs_5_.refs_4_.refs_2_), channel_id=1, source_target_pairs={{0,6},{8,10},{2,0},{10,12},{4,2},{12,14},{6,4},{14,8},{1,7},{9,11}... | collective-permute-start | bytes 2654216 | tf_op jit(solution)/shard_map/two/ppermute | solution.py:377
  13.3 58.3 %all-to-all-start = ((bf16[4,384,1152]{2,1,0:T(8,128)(2,1)}), bf16[4,384,1152]{2,1,0:T(8,128)(2,1)S(1)}, u32[]{:S(2)}, u32[]{:S(2)}) async-start(bf16[4,384,1152]{2,1,0:T(8,128)(2,1)} %get-tuple-element.21), calls=%async_computation | async-start | bytes 7077888 | tf_op jit(solution)/shard_map/turns/all_to_all | solution.py:394
  20.5 30.8 %collective-permute-start.5 = (bf16[384,1152]{1,0:T(8,128)(2,1)}, bf16[384,1152]{1,0:T(8,128)(2,1)}, u32[]{:S(2)}, u32[]{:S(2)}) collective-permute-start(bf16[384,1152]{1,0:T(8,128)(2,1)} %collective-permute-done.4.refs_3_.refs_2_), channel_id=1, source_target_pairs={{0,2},{8,14},{2,4},{10,8},{4,6},{12,10},{6,0},{14,12},{1,3},{9,15}... | collective-permute-start | bytes 2654216 | tf_op jit(solution)/shard_map/opp/ppermute | solution.py:377
  27.8 59.8 %collective-permute-start.2 = (bf16[384,1152]{1,0:T(8,128)(2,1)}, bf16[384,1152]{1,0:T(8,128)(2,1)}, u32[]{:S(2)}, u32[]{:S(2)}) collective-permute-start(bf16[384,1152]{1,0:T(8,128)(2,1)} %gate.3.refs_6_), channel_id=1, source_target_pairs={{48,64},{0,240},{8,72},{56,248},{112,128},{64,48},{72,136},{120,56... | collective-permute-start | bytes 2654216 | tf_op jit(solution)/shard_map/over_a/ppermute | solution.py:404
  29.4 58.3 %collective-permute-start.9 = (bf16[384,1152]{1,0:T(8,128)(2,1)}, bf16[384,1152]{1,0:T(8,128)(2,1)}, u32[]{:S(2)}, u32[]{:S(2)}) collective-permute-start(bf16[384,1152]{1,0:T(8,128)(2,1)} %gate.3.refs_6_), channel_id=1, source_target_pairs={{32,64},{16,240},{24,72},{40,248},{96,128},{80,48},{88,136},{104,5... | collective-permute-start | bytes 2654216 | tf_op jit(solution)/shard_map/over_b/ppermute | solution.py:404
  49.9 42.6 %collective-permute-start.12 = (bf16[384,1152]{1,0:T(8,128)(2,1)}, bf16[384,1152]{1,0:T(8,128)(2,1)}, u32[]{:S(2)}, u32[]{:S(2)}) collective-permute-start(bf16[384,1152]{1,0:T(8,128)(2,1)} %get-tuple-element.22.refs_4_), channel_id=1, source_target_pairs={{0,6},{8,10},{2,0},{10,12},{4,2},{12,14},{6,4},{14,8},{1,7},{9,11}... | collective-permute-start | bytes 2654216 | tf_op jit(solution)/shard_map/early/ppermute | solution.py:377
  56.8 31.0 %collective-permute-start.11 = (bf16[384,1152]{1,0:T(8,128)(2,1)}, bf16[384,1152]{1,0:T(8,128)(2,1)}, u32[]{:S(2)}, u32[]{:S(2)}) collective-permute-start(bf16[384,1152]{1,0:T(8,128)(2,1)} %get-tuple-element.23.after_ref), channel_id=1, source_target_pairs={{0,2},{8,14},{2,4},{10,8},{4,6},{12,10},{6,0},{14,12},{1,3},{9,15}... | collective-permute-start | bytes 2654216 | tf_op jit(solution)/shard_map/carried/ppermute | solution.py:377
  71.6 1.8 %copy-start = (bf16[4,384,1152]{2,1,0:T(8,128)(2,1)}, bf16[4,384,1152]{2,1,0:T(8,128)(2,1)S(1)}, u32[]{:S(2)}) copy-start(bf16[4,384,1152]{2,1,0:T(8,128)(2,1)S(1)} %all-to-all-done.block_ref) | copy-start | bytes 10616836
  73.4 23.0 %collective-permute-start.7 = (bf16[4,384,1152]{2,1,0:T(8,128)(2,1)}, bf16[4,384,1152]{2,1,0:T(8,128)(2,1)}, u32[]{:S(2)}, u32[]{:S(2)}) collective-permute-start(bf16[4,384,1152]{2,1,0:T(8,128)(2,1)} %gate.4.refs_3_), channel_id=1, source_target_pairs={{0,8},{8,0},{1,9},{9,1},{2,10},{10,2},{3,11},{11,3},{4,12},{12,4},... | collective-permute-start | bytes 10616840 | tf_op jit(solution)/shard_map/sib/ppermute | solution.py:27
  87.6 33.8 %collective-permute-start.14 = (bf16[384,1152]{1,0:T(8,128)(2,1)}, bf16[384,1152]{1,0:T(8,128)(2,1)S(1)}, u32[]{:S(2)}, u32[]{:S(2)}) collective-permute-start(bf16[384,1152]{1,0:T(8,128)(2,1)} %get-tuple-element.29.refs_2_), channel_id=1, source_target_pairs={{0,1},{1,0},{2,3},{3,2},{4,5},{5,4},{6,7},{7,6},{8,9},{9,8},{10,11... | collective-permute-start | bytes 2654216 | tf_op jit(solution)/shard_map/back/ppermute | solution.py:27
  87.7 6.1 %collective-permute-start.8 = (bf16[384,1152]{1,0:T(8,128)(2,1)}, bf16[384,1152]{1,0:T(8,128)(2,1)S(1)}, u32[]{:S(2)}, u32[]{:S(2)}) collective-permute-start(bf16[384,1152]{1,0:T(8,128)(2,1)} %collective-permute-done.2.refs_5_), channel_id=1, source_target_pairs={{0,8},{8,0},{1,9},{9,1},{2,10},{10,2},{3,11},{11,3},{4,12},{12,4},... | collective-permute-start | bytes 2654216 | tf_op jit(solution)/shard_map/over_a1/ppermute | solution.py:27
  87.9 8.5 %collective-permute-start.10 = (bf16[384,1152]{1,0:T(8,128)(2,1)}, bf16[384,1152]{1,0:T(8,128)(2,1)}, u32[]{:S(2)}, u32[]{:S(2)}) collective-permute-start(bf16[384,1152]{1,0:T(8,128)(2,1)} %collective-permute-done.9.refs_7_), channel_id=1, source_target_pairs={{8,0},{48,56},{9,1},{49,57},{10,2},{50,58},{11,3},{51,59},{12,4},{... | collective-permute-start | bytes 2654216 | tf_op jit(solution)/shard_map/over_b1/ppermute | solution.py:459
  92.5 26.5 %collective-permute-start.3 = (bf16[384,1152]{1,0:T(8,128)(2,1)}, bf16[384,1152]{1,0:T(8,128)(2,1)S(1)}, u32[]{:S(2)}, u32[]{:S(2)}) collective-permute-start(bf16[384,1152]{1,0:T(8,128)(2,1)} %collective-permute-done.2.refs_5_), channel_id=1, source_target_pairs={{0,16},{48,32},{1,17},{49,33},{2,18},{50,34},{3,19},{51,35},{4,20}... | collective-permute-start | bytes 2654216 | tf_op jit(solution)/shard_map/over_f/ppermute | solution.py:455
  93.8 2.6 %copy-start.4 = (bf16[384,1152]{1,0:T(8,128)(2,1)}, bf16[384,1152]{1,0:T(8,128)(2,1)S(1)}, u32[]{:S(2)}) copy-start(bf16[384,1152]{1,0:T(8,128)(2,1)S(1)} %collective-permute-done.8.refs_6_) | copy-start | bytes 2654212
  93.8 27.6 %collective-permute-start.15 = (bf16[384,1152]{1,0:T(8,128)(2,1)}, bf16[384,1152]{1,0:T(8,128)(2,1)S(1)}, u32[]{:S(2)}, u32[]{:S(2)}) collective-permute-start(bf16[384,1152]{1,0:T(8,128)(2,1)} %add.1.refs_11_), channel_id=1, source_target_pairs={{0,2},{8,14},{2,4},{10,8},{4,6},{12,10},{6,0},{14,12},{1,3},{9,15}... | collective-permute-start | bytes 2654216 | tf_op jit(solution)/shard_map/late/ppermute | solution.py:377
  119.1 1.0 copy-start.1
  120.0 3.5 %collective-permute-start.13 = (bf16[384,1152]{1,0:T(8,128)(2,1)}, bf16[384,1152]{1,0:T(8,128)(2,1)S(1)}, u32[]{:S(2)}, u32[]{:S(2)}) collective-permute-start(bf16[384,1152]{1,0:T(8,128)(2,1)} %gate.5.refs_1_), channel_id=1, source_target_pairs={{24,16},{32,40},{25,17},{33,41},{26,18},{34,42},{27,19},{35,43},{2... | collective-permute-start | bytes 2654216 | tf_op jit(solution)/shard_map/over_f1/ppermute | solution.py:474
  121.4 2.2 %copy-start.2 = (bf16[384,1152]{1,0:T(8,128)(2,1)}, bf16[384,1152]{1,0:T(8,128)(2,1)S(1)}, u32[]{:S(2)}) copy-start(bf16[384,1152]{1,0:T(8,128)(2,1)S(1)} %collective-permute-done.14.refs_7_) | copy-start | bytes 2654212
  121.4 2.2 %copy-start.3 = (bf16[384,1152]{1,0:T(8,128)(2,1)}, bf16[384,1152]{1,0:T(8,128)(2,1)S(1)}, u32[]{:S(2)}) copy-start(bf16[384,1152]{1,0:T(8,128)(2,1)S(1)} %collective-permute-done.15.refs_11_) | copy-start | bytes 2654212
  123.6 0.9 copy-start.5

commit v3 on v2

--- a/solution.py
+++ b/solution.py
@@ -37,7 +37,7 @@
         in_specs=[SM] * smem + [ANY] * (len(args) - smem),
         out_specs=[ANY] * len(outs),
         scratch_shapes=list(scratch) + [pltpu.SemaphoreType.DMA((32,))],
-        cost_estimate=pl.CostEstimate(flops=20_000_000_000, bytes_accessed=0, transcendentals=0),
+        cost_estimate=pl.CostEstimate(flops=1 if name in ("opposite", "image_side") else 20_000_000_000, bytes_accessed=0, transcendentals=0),
         compiler_params=pltpu.CompilerParams(vmem_limit_bytes=60 * 2**20),
         name=name,
     )(*args)
@@ -214,7 +214,8 @@
 
 
 def image_kernel(
-    copies, wt3_ref, wt_ref, one_ref, two_ref, text_ref, opp_ref, far_out, near_out,
+    copies, wt3_ref, wt_ref, one_ref, two_ref, text_ref, opp_ref, after_ref, then_ref, again_ref,
+    far_out, near_out,
     w_scr, t_scr, far, near,
 ):
     come = [
@@ -283,7 +284,7 @@
         copy.wait()
 
 
-def add_kernel(copies, late_ref, return_ref, after_ref, out_ref, late, back, out):
+def add_kernel(copies, late_ref, return_ref, after_ref, then_ref, out_ref, late, back, out):
     come = [copies.go(late_ref, late), copies.go(return_ref, back)]
     for copy in come:
         copy.wait()
@@ -429,22 +430,22 @@
     )
     with jax.named_scope("carried"):
         carried = along_y(part_opp, 1)
-    own = gate(own, part_opp)
-    with jax.named_scope("sib"):
-        sib = ring(own, "c", 1)
     grad_far, grad_image = call(
         image_kernel,
         [WHOLE, WHOLE32],
-        (wt3, wt, text_one, text_two, text, text_opp),
+        (wt3, wt, text_one, text_two, text, text_opp, over_a, over_b, carried),
         [vm(4 * ROWS, 2 * ROWS), vm(4 * ROWS), vm(ROWS), vm(ROWS, dtype=F32)],
         "image_side",
     )
     with jax.named_scope("back"):
         grad_back = ring(grad_far, "zl", 1)
+    own = gate(own, grad_far)
+    with jax.named_scope("sib"):
+        sib = ring(own, "c", 1)
     part_late = call(
         add_kernel,
         [WHOLE],
-        (part_late, carried, grad_far),
+        (part_late, carried, grad_far, early),
         [vm(ROWS, dtype=F32), vm(ROWS), vm(ROWS)],
         "add",
     )[0]

time: 134 us -> 130 us (0.970)
  the two profiles are of different devices: /device:TPU:3 before, /device:TPU:1 now
where the time goes in v3:
time: 130 us
  Pallas kernels  50.9 us (39%)
  waiting for transfers between devices  36.1 us (28%)
  starting transfers between devices  34.1 us (26%)
  local copies, waits for them, and re-layouts  5.58 us (4%)
  between operations  2.31 us (2%)
    pallas_call x7, Pallas kernels, call(): pl.pallas_call(kernel, out_shape=[jax.ShapeDtypeStruct(s, d) for s, d in...  50.9 us
    ppermute x6, waiting for transfers between devices, along_y(): return lax.ppermute(block, ('c', 'y'), pairs)  16.2 us
    all_to_all x1, waiting for transfers between devices, local(): own = lax.all_to_all(turns, 'x', split_axis=0, concat_axis=0, tiled=True)  10.5 us
    ppermute x6, starting transfers between devices, along_y(): return lax.ppermute(block, ('c', 'y'), pairs)  9.02 us
    ppermute x2, starting transfers between devices, over(): return lax.ppermute(hop, GROUP, sends)  7.12 us
    unnamed x14, local copies, waits for them, and re-layouts  5.58 us
    ppermute x4, starting transfers between devices, ring(): return lax.ppermute(x, axis, [(i, (i + by) % size) for i in range(size)])  4.97 us
    ppermute x4, waiting for transfers between devices, ring(): return lax.ppermute(x, axis, [(i, (i + by) % size) for i in range(size)])  4.54 us
  transfers between devices with their start and end apart: 17, of which 8 were waited for; matrix products, arithmetic and copies ran while one was open for 0% of the time, Pallas kernels for 29%

profile of v3, /device:TPU:1, one launch (start us, length us, event | category | flops | bytes accessed | tf_op | source)
XLA Modules:
  0.0 129.6 jit_solution(10103107672095801512)
XLA Ops:
  0.6 5.0 %unit.1 = (bf16[384,1152]{1,0:T(8,128)(2,1)}, bf16[400,1152]{1,0:T(8,128)(2,1)}, bf16[384,1152]{1,0:T(8,128)(2,1)}, bf16[4,384,1152]{2,1,0:T(8,128)(2,1)}) custom-call(s32[2,8]{1,0:T(2,128)} %bitcast.15, bf16[384,1152]{1,0:T(8,128)(2,1)} %bitcast.11, bf16[384,1152]{1,0:T(8,128)(2,1)} %bitcast.13), custom_call_target="tpu_custom_call" | custom-call | flops 20000000000 | tf_op jit(solution)/shard_map/unit/pallas_call | solution.py:34
  5.7 2.6 %collective-permute-start.1 = (bf16[400,1152]{1,0:T(8,128)(2,1)}, bf16[400,1152]{1,0:T(8,128)(2,1)}, u32[]{:S(2)}, u32[]{:S(2)}) collective-permute-start(bf16[400,1152]{1,0:T(8,128)(2,1)} %get-tuple-element.19.refs_1_.refs_3_), channel_id=1, source_target_pairs={{0,1},{1,0},{2,3},{3,2},{4,5},{5,4},{6,7},{7,6},{8,9},{9,8},{10,11... | collective-permute-start | bytes 2764808 | tf_op jit(solution)/shard_map/other/ppermute | solution.py:27
  8.2 2.7 %collective-permute-start.4 = (bf16[384,1152]{1,0:T(8,128)(2,1)}, bf16[384,1152]{1,0:T(8,128)(2,1)}, u32[]{:S(2)}, u32[]{:S(2)}) collective-permute-start(bf16[384,1152]{1,0:T(8,128)(2,1)} %get-tuple-element.20.refs_5_.refs_4_.refs_2_), channel_id=1, source_target_pairs={{0,2},{8,14},{2,4},{10,8},{4,6},{12,10},{6,0},{14,12},{1,3},{9,15}... | collective-permute-start | bytes 2654216 | tf_op jit(solution)/shard_map/one/ppermute | solution.py:378
  10.9 4.4 %collective-permute-start = (bf16[384,1152]{1,0:T(8,128)(2,1)}, bf16[384,1152]{1,0:T(8,128)(2,1)}, u32[]{:S(2)}, u32[]{:S(2)}) collective-permute-start(bf16[384,1152]{1,0:T(8,128)(2,1)} %get-tuple-element.18), channel_id=1, source_target_pairs={{0,0},{16,16},{32,32},{48,48},{56,8},{40,24},{24,40},{8,56},{1,1},... | collective-permute-start | bytes 2654216 | tf_op jit(solution)/shard_map/hop/ppermute | solution.py:388
  15.4 3.7 %all-to-all-start = ((bf16[4,384,1152]{2,1,0:T(8,128)(2,1)}), bf16[4,384,1152]{2,1,0:T(8,128)(2,1)S(1)}, u32[]{:S(2)}, u32[]{:S(2)}) async-start(bf16[4,384,1152]{2,1,0:T(8,128)(2,1)} %get-tuple-element.21), calls=%async_computation | async-start | bytes 7077888 | tf_op jit(solution)/shard_map/turns/all_to_all | solution.py:395
  21.3 3.1 %collective-permute-start.6 = (bf16[384,1152]{1,0:T(8,128)(2,1)}, bf16[384,1152]{1,0:T(8,128)(2,1)}, u32[]{:S(2)}, u32[]{:S(2)}) collective-permute-start(bf16[384,1152]{1,0:T(8,128)(2,1)} %collective-permute-done.4.refs_3_.refs_2_), channel_id=1, source_target_pairs={{0,2},{8,14},{2,4},{10,8},{4,6},{12,10},{6,0},{14,12},{1,3},{9,15}... | collective-permute-start | bytes 2654216 | tf_op jit(solution)/shard_map/opp/ppermute | solution.py:378
  24.4 2.2 %collective-permute-done.block_ref = bf16[384,1152]{1,0:T(8,128)(2,1)} collective-permute-done((bf16[384,1152]{1,0:T(8,128)(2,1)}, bf16[384,1152]{1,0:T(8,128)(2,1)}, u32[]{:S(2)}, u32[]{:S(2)}) %collective-permute-start) | collective-permute-done | bytes 884768 | tf_op jit(solution)/shard_map/hop/ppermute | solution.py:388
  27.6 5.8 %collective-permute-start.2 = (bf16[384,1152]{1,0:T(8,128)(2,1)}, bf16[384,1152]{1,0:T(8,128)(2,1)}, u32[]{:S(2)}, u32[]{:S(2)}) collective-permute-start(bf16[384,1152]{1,0:T(8,128)(2,1)} %gate.3.refs_6_), channel_id=1, source_target_pairs={{48,64},{0,240},{8,72},{56,248},{112,128},{64,48},{72,136},{120,56... | collective-permute-start | bytes 2654216 | tf_op jit(solution)/shard_map/over_a/ppermute | solution.py:405
  34.8 10.6 %hard.1 = (bf16[384,1152]{1,0:T(8,128)(2,1)}, f32[384,1152]{1,0:T(8,128)}, f32[384,1152]{1,0:T(8,128)}, bf16[1152,768]{1,0:T(8,128)(2,1)}) custom-call(f32[2]{0:T(128)} %pad_maximum_fusion.refs_0_, bf16[400,1152]{1,0:T(8,128)(2,1)} %get-tuple-element.19.refs_1_.refs_3_, bf16[400,1152]{1,0:T(8,128)(2,1)} %collective-permute-done.1.after_ref.refs_2_, ...), custom_call_target="tpu_custom_call" | custom-call | flops 20000000000 | tf_op jit(solution)/shard_map/hard/pallas_call | solution.py:34
  45.4 5.5 %opposite.1 = (bf16[384,1152]{1,0:T(8,128)(2,1)}, bf16[384,768]{1,0:T(8,128)(2,1)}) custom-call(f32[2]{0:T(128)} %pad_maximum_fusion.refs_0_, bf16[400,1152]{1,0:T(8,128)(2,1)} %get-tuple-element.19.refs_1_.refs_3_, bf16[400,1152]{1,0:T(8,128)(2,1)} %collective-permute-done.1.after_ref.refs_2_, bf16[384,1152]{1,0:T(8,128)(2,1)} %collective-permute-done.6.refs_3_.refs_5_, ...), custom_call_target="tpu_custom_call" | custom-call | flops 1 | tf_op jit(solution)/shard_map/opposite/pallas_call | solution.py:34
  50.9 3.0 %collective-permute-start.8 = (bf16[384,1152]{1,0:T(8,128)(2,1)}, bf16[384,1152]{1,0:T(8,128)(2,1)}, u32[]{:S(2)}, u32[]{:S(2)}) collective-permute-start(bf16[384,1152]{1,0:T(8,128)(2,1)} %get-tuple-element.25), channel_id=1, source_target_pairs={{0,2},{8,14},{2,4},{10,8},{4,6},{12,10},{6,0},{14,12},{1,3},{9,15}... | collective-permute-start | bytes 2654216 | tf_op jit(solution)/shard_map/carried/ppermute | solution.py:378
  53.9 2.7 %collective-permute-done.7.refs_7_ = bf16[384,1152]{1,0:T(8,128)(2,1)} collective-permute-done((bf16[384,1152]{1,0:T(8,128)(2,1)}, bf16[384,1152]{1,0:T(8,128)(2,1)}, u32[]{:S(2)}, u32[]{:S(2)}) %collective-permute-start.7) | collective-permute-done | bytes 884768 | tf_op jit(solution)/shard_map/over_b/ppermute | solution.py:405
  56.6 7.6 %collective-permute-done.8.refs_8_.refs_1_ = bf16[384,1152]{1,0:T(8,128)(2,1)} collective-permute-done((bf16[384,1152]{1,0:T(8,128)(2,1)}, bf16[384,1152]{1,0:T(8,128)(2,1)}, u32[]{:S(2)}, u32[]{:S(2)}) %collective-permute-start.8) | collective-permute-done | bytes 884768 | tf_op jit(solution)/shard_map/carried/ppermute | solution.py:378
  64.2 7.5 %image_side.1 = (bf16[384,1152]{1,0:T(8,128)(2,1)}, f32[384,1152]{1,0:T(8,128)}) custom-call(bf16[1152,768]{1,0:T(8,128)(2,1)} %get-tuple-element.22.refs_0_, bf16[384,768]{1,0:T(8,128)(2,1)} %get-tuple-element.24.refs_1_, bf16[384,1152]{1,0:T(8,128)(2,1)} %collective-permute-done.4.refs_3_.refs_2_, ...), custom_call_target="tpu_custom_call" | custom-call | flops 1 | tf_op jit(solution)/shard_map/image_side/pallas_call | solution.py:34
  71.7 10.5 %all-to-all-done.block_ref = bf16[4,384,1152]{2,1,0:T(8,128)(2,1)S(1)} async-done(((bf16[4,384,1152]{2,1,0:T(8,128)(2,1)}), bf16[4,384,1152]{2,1,0:T(8,128)(2,1)S(1)}, u32[]{:S(2)}, u32[]{:S(2)}) %all-to-all-start) | async-done | bytes 3538976 | tf_op jit(solution)/shard_map/turns/all_to_all | solution.py:395
  82.1 1.8 %copy-done = bf16[4,384,1152]{2,1,0:T(8,128)(2,1)} copy-done((bf16[4,384,1152]{2,1,0:T(8,128)(2,1)}, bf16[4,384,1152]{2,1,0:T(8,128)(2,1)S(1)}, u32[]{:S(2)}) %copy-start) | copy-done | bytes 3538968
  84.0 1.6 %collective-permute-start.9 = (bf16[4,384,1152]{2,1,0:T(8,128)(2,1)}, bf16[4,384,1152]{2,1,0:T(8,128)(2,1)}, u32[]{:S(2)}, u32[]{:S(2)}) collective-permute-start(bf16[4,384,1152]{2,1,0:T(8,128)(2,1)} %gate.4.refs_3_), channel_id=1, source_target_pairs={{0,8},{8,0},{1,9},{9,1},{2,10},{10,2},{3,11},{11,3},{4,12},{12,4},... | collective-permute-start | bytes 10616840 | tf_op jit(solution)/shard_map/sib/ppermute | solution.py:27
  86.3 2.8 %collective-permute-start.11 = (bf16[384,1152]{1,0:T(8,128)(2,1)}, bf16[384,1152]{1,0:T(8,128)(2,1)}, u32[]{:S(2)}, u32[]{:S(2)}) collective-permute-start(bf16[384,1152]{1,0:T(8,128)(2,1)} %collective-permute-done.7.refs_7_), channel_id=1, source_target_pairs={{8,0},{48,56},{9,1},{49,57},{10,2},{50,58},{11,3},{51,59},{12,4},{... | collective-permute-start | bytes 2654216 | tf_op jit(solution)/shard_map/over_b1/ppermute | solution.py:460
  89.1 1.3 %collective-permute-start.3 = (bf16[384,1152]{1,0:T(8,128)(2,1)}, bf16[384,1152]{1,0:T(8,128)(2,1)S(1)}, u32[]{:S(2)}, u32[]{:S(2)}) collective-permute-start(bf16[384,1152]{1,0:T(8,128)(2,1)} %collective-permute-done.2.refs_6_.refs_5_), channel_id=1, source_target_pairs={{0,16},{48,32},{1,17},{49,33},{2,18},{50,34},{3,19},{51,35},{4,20}... | collective-permute-start | bytes 2654216 | tf_op jit(solution)/shard_map/over_f/ppermute | solution.py:456
  90.4 8.4 %collective-permute-done.12.refs_3_.refs_12_.refs_10_ = bf16[384,1152]{1,0:T(8,128)(2,1)S(1)} collective-permute-done((bf16[384,1152]{1,0:T(8,128)(2,1)}, bf16[384,1152]{1,0:T(8,128)(2,1)S(1)}, u32[]{:S(2)}, u32[]{:S(2)}) %collective-permute-start.12) | collective-permute-done | bytes 884768 | tf_op jit(solution)/shard_map/early/ppermute | solution.py:378
  99.8 3.0 %add.1.refs_11_ = bf16[384,1152]{1,0:T(8,128)(2,1)} custom-call(f32[384,1152]{1,0:T(8,128)} %get-tuple-element.29.refs_0_, bf16[384,1152]{1,0:T(8,128)(2,1)} %collective-permute-done.8.refs_8_.refs_1_, bf16[384,1152]{1,0:T(8,128)(2,1)} %get-tuple-element.26.after_ref.refs_2_, bf16[384,1152]{1,0:T(8,128)(2,1)} %copy-done.2), custom_call_target="tpu_custom_call" | custom-call | flops 20000000000 | tf_op jit(solution)/shard_map/add/pallas_call | solution.py:34
  103.8 11.5 %cycle.1 = (f32[384,1152]{1,0:T(8,128)}, f32[384,1152]{1,0:T(8,128)}) custom-call(f32[2]{0:T(128)} %pad_maximum_fusion.refs_0_, bf16[400,1152]{1,0:T(8,128)(2,1)} %get-tuple-element.19.refs_1_.refs_3_, bf16[384,1152]{1,0:T(8,128)(2,1)} %get-tuple-element.20.refs_5_.refs_4_.refs_2_, bf16[4,384,1152]{2,1,0:T(8,128)(2,1)} %gate.4.refs_3_, ...), custom_call_target="tpu_custom_call" | custom-call | flops 20000000000 | tf_op jit(solution)/shard_map/cycle/pallas_call | solution.py:34
  117.0 3.5 %collective-permute-done.14.refs_7_ = bf16[384,1152]{1,0:T(8,128)(2,1)S(1)} collective-permute-done((bf16[384,1152]{1,0:T(8,128)(2,1)}, bf16[384,1152]{1,0:T(8,128)(2,1)S(1)}, u32[]{:S(2)}, u32[]{:S(2)}) %collective-permute-start.14) | collective-permute-done | bytes 884768 | tf_op jit(solution)/shard_map/back/ppermute | solution.py:27
  121.6 7.7 %last.1 = (f32[384,1152]{1,0:T(8,128)}, f32[384,1152]{1,0:T(8,128)}) custom-call(f32[2]{0:T(128)} %pad_maximum_fusion.refs_0_, bf16[384,1152]{1,0:T(8,128)(2,1)} %gate.5.refs_1_, bf16[384,1152]{1,0:T(8,128)(2,1)} %copy-done.6, bf16[400,1152]{1,0:T(8,128)(2,1)} %get-tuple-element.19.refs_1_.refs_3_, ...), custom_call_target="tpu_custom_call" | custom-call | flops 20000000000 | tf_op jit(solution)/shard_map/last/pallas_call | solution.py:34
  (35 shorter events, 8.7 us)
Async XLA Ops:
  5.7 22.0 %collective-permute-start.1 = (bf16[400,1152]{1,0:T(8,128)(2,1)}, bf16[400,1152]{1,0:T(8,128)(2,1)}, u32[]{:S(2)}, u32[]{:S(2)}) collective-permute-start(bf16[400,1152]{1,0:T(8,128)(2,1)} %get-tuple-element.19.refs_1_.refs_3_), channel_id=1, source_target_pairs={{0,1},{1,0},{2,3},{3,2},{4,5},{5,4},{6,7},{7,6},{8,9},{9,8},{10,11... | collective-permute-start | bytes 2764808 | tf_op jit(solution)/shard_map/other/ppermute | solution.py:27
  8.2 13.0 %collective-permute-start.4 = (bf16[384,1152]{1,0:T(8,128)(2,1)}, bf16[384,1152]{1,0:T(8,128)(2,1)}, u32[]{:S(2)}, u32[]{:S(2)}) collective-permute-start(bf16[384,1152]{1,0:T(8,128)(2,1)} %get-tuple-element.20.refs_5_.refs_4_.refs_2_), channel_id=1, source_target_pairs={{0,2},{8,14},{2,4},{10,8},{4,6},{12,10},{6,0},{14,12},{1,3},{9,15}... | collective-permute-start | bytes 2654216 | tf_op jit(solution)/shard_map/one/ppermute | solution.py:378
  10.9 15.6 %collective-permute-start = (bf16[384,1152]{1,0:T(8,128)(2,1)}, bf16[384,1152]{1,0:T(8,128)(2,1)}, u32[]{:S(2)}, u32[]{:S(2)}) collective-permute-start(bf16[384,1152]{1,0:T(8,128)(2,1)} %get-tuple-element.18), channel_id=1, source_target_pairs={{0,0},{16,16},{32,32},{48,48},{56,8},{40,24},{24,40},{8,56},{1,1},... | collective-permute-start | bytes 2654216 | tf_op jit(solution)/shard_map/hop/ppermute | solution.py:388
  15.3 19.4 %collective-permute-start.5 = (bf16[384,1152]{1,0:T(8,128)(2,1)}, bf16[384,1152]{1,0:T(8,128)(2,1)}, u32[]{:S(2)}, u32[]{:S(2)}) collective-permute-start(bf16[384,1152]{1,0:T(8,128)(2,1)} %get-tuple-element.20.refs_5_.refs_4_.refs_2_), channel_id=1, source_target_pairs={{0,6},{8,10},{2,0},{10,12},{4,2},{12,14},{6,4},{14,8},{1,7},{9,11}... | collective-permute-start | bytes 2654216 | tf_op jit(solution)/shard_map/two/ppermute | solution.py:378
  15.4 66.7 %all-to-all-start = ((bf16[4,384,1152]{2,1,0:T(8,128)(2,1)}), bf16[4,384,1152]{2,1,0:T(8,128)(2,1)S(1)}, u32[]{:S(2)}, u32[]{:S(2)}) async-start(bf16[4,384,1152]{2,1,0:T(8,128)(2,1)} %get-tuple-element.21), calls=%async_computation | async-start | bytes 7077888 | tf_op jit(solution)/shard_map/turns/all_to_all | solution.py:395
  21.3 24.1 %collective-permute-start.6 = (bf16[384,1152]{1,0:T(8,128)(2,1)}, bf16[384,1152]{1,0:T(8,128)(2,1)}, u32[]{:S(2)}, u32[]{:S(2)}) collective-permute-start(bf16[384,1152]{1,0:T(8,128)(2,1)} %collective-permute-done.4.refs_3_.refs_2_), channel_id=1, source_target_pairs={{0,2},{8,14},{2,4},{10,8},{4,6},{12,10},{6,0},{14,12},{1,3},{9,15}... | collective-permute-start | bytes 2654216 | tf_op jit(solution)/shard_map/opp/ppermute | solution.py:378
  27.6 26.3 %collective-permute-start.2 = (bf16[384,1152]{1,0:T(8,128)(2,1)}, bf16[384,1152]{1,0:T(8,128)(2,1)}, u32[]{:S(2)}, u32[]{:S(2)}) collective-permute-start(bf16[384,1152]{1,0:T(8,128)(2,1)} %gate.3.refs_6_), channel_id=1, source_target_pairs={{48,64},{0,240},{8,72},{56,248},{112,128},{64,48},{72,136},{120,56... | collective-permute-start | bytes 2654216 | tf_op jit(solution)/shard_map/over_a/ppermute | solution.py:405
  33.5 23.1 %collective-permute-start.7 = (bf16[384,1152]{1,0:T(8,128)(2,1)}, bf16[384,1152]{1,0:T(8,128)(2,1)}, u32[]{:S(2)}, u32[]{:S(2)}) collective-permute-start(bf16[384,1152]{1,0:T(8,128)(2,1)} %gate.3.refs_6_), channel_id=1, source_target_pairs={{32,64},{16,240},{24,72},{40,248},{96,128},{80,48},{88,136},{104,5... | collective-permute-start | bytes 2654216 | tf_op jit(solution)/shard_map/over_b/ppermute | solution.py:405
  50.9 13.3 %collective-permute-start.8 = (bf16[384,1152]{1,0:T(8,128)(2,1)}, bf16[384,1152]{1,0:T(8,128)(2,1)}, u32[]{:S(2)}, u32[]{:S(2)}) collective-permute-start(bf16[384,1152]{1,0:T(8,128)(2,1)} %get-tuple-element.25), channel_id=1, source_target_pairs={{0,2},{8,14},{2,4},{10,8},{4,6},{12,10},{6,0},{14,12},{1,3},{9,15}... | collective-permute-start | bytes 2654216 | tf_op jit(solution)/shard_map/carried/ppermute | solution.py:378
  82.1 1.8 %copy-start = (bf16[4,384,1152]{2,1,0:T(8,128)(2,1)}, bf16[4,384,1152]{2,1,0:T(8,128)(2,1)S(1)}, u32[]{:S(2)}) copy-start(bf16[4,384,1152]{2,1,0:T(8,128)(2,1)S(1)} %all-to-all-done.block_ref) | copy-start | bytes 10616836
  84.0 19.0 %collective-permute-start.9 = (bf16[4,384,1152]{2,1,0:T(8,128)(2,1)}, bf16[4,384,1152]{2,1,0:T(8,128)(2,1)}, u32[]{:S(2)}, u32[]{:S(2)}) collective-permute-start(bf16[4,384,1152]{2,1,0:T(8,128)(2,1)} %gate.4.refs_3_), channel_id=1, source_target_pairs={{0,8},{8,0},{1,9},{9,1},{2,10},{10,2},{3,11},{11,3},{4,12},{12,4},... | collective-permute-start | bytes 10616840 | tf_op jit(solution)/shard_map/sib/ppermute | solution.py:27
  85.5 13.3 %collective-permute-start.12 = (bf16[384,1152]{1,0:T(8,128)(2,1)}, bf16[384,1152]{1,0:T(8,128)(2,1)S(1)}, u32[]{:S(2)}, u32[]{:S(2)}) collective-permute-start(bf16[384,1152]{1,0:T(8,128)(2,1)} %get-tuple-element.23.refs_4_), channel_id=1, source_target_pairs={{0,6},{8,10},{2,0},{10,12},{4,2},{12,14},{6,4},{14,8},{1,7},{9,11}... | collective-permute-start | bytes 2654216 | tf_op jit(solution)/shard_map/early/ppermute | solution.py:378
  85.5 17.3 %collective-permute-start.10 = (bf16[384,1152]{1,0:T(8,128)(2,1)}, bf16[384,1152]{1,0:T(8,128)(2,1)S(1)}, u32[]{:S(2)}, u32[]{:S(2)}) collective-permute-start(bf16[384,1152]{1,0:T(8,128)(2,1)} %collective-permute-done.2.refs_6_.refs_5_), channel_id=1, source_target_pairs={{0,8},{8,0},{1,9},{9,1},{2,10},{10,2},{3,11},{11,3},{4,12},{12,4},... | collective-permute-start | bytes 2654216 | tf_op jit(solution)/shard_map/over_a1/ppermute | solution.py:27
  86.3 16.7 %collective-permute-start.11 = (bf16[384,1152]{1,0:T(8,128)(2,1)}, bf16[384,1152]{1,0:T(8,128)(2,1)}, u32[]{:S(2)}, u32[]{:S(2)}) collective-permute-start(bf16[384,1152]{1,0:T(8,128)(2,1)} %collective-permute-done.7.refs_7_), channel_id=1, source_target_pairs={{8,0},{48,56},{9,1},{49,57},{10,2},{50,58},{11,3},{51,59},{12,4},{... | collective-permute-start | bytes 2654216 | tf_op jit(solution)/shard_map/over_b1/ppermute | solution.py:460
  89.1 26.2 %collective-permute-start.3 = (bf16[384,1152]{1,0:T(8,128)(2,1)}, bf16[384,1152]{1,0:T(8,128)(2,1)S(1)}, u32[]{:S(2)}, u32[]{:S(2)}) collective-permute-start(bf16[384,1152]{1,0:T(8,128)(2,1)} %collective-permute-done.2.refs_6_.refs_5_), channel_id=1, source_target_pairs={{0,16},{48,32},{1,17},{49,33},{2,18},{50,34},{3,19},{51,35},{4,20}... | collective-permute-start | bytes 2654216 | tf_op jit(solution)/shard_map/over_f/ppermute | solution.py:456
  98.8 0.9 copy-start.2
  98.8 21.6 %collective-permute-start.14 = (bf16[384,1152]{1,0:T(8,128)(2,1)}, bf16[384,1152]{1,0:T(8,128)(2,1)S(1)}, u32[]{:S(2)}, u32[]{:S(2)}) collective-permute-start(bf16[384,1152]{1,0:T(8,128)(2,1)} %get-tuple-element.26.after_ref.refs_2_), channel_id=1, source_target_pairs={{0,1},{1,0},{2,3},{3,2},{4,5},{5,4},{6,7},{7,6},{8,9},{9,8},{10,11... | collective-permute-start | bytes 2654216 | tf_op jit(solution)/shard_map/back/ppermute | solution.py:27
  102.8 0.9 copy-start.5
  102.8 14.1 %collective-permute-start.15 = (bf16[384,1152]{1,0:T(8,128)(2,1)}, bf16[384,1152]{1,0:T(8,128)(2,1)S(1)}, u32[]{:S(2)}, u32[]{:S(2)}) collective-permute-start(bf16[384,1152]{1,0:T(8,128)(2,1)} %add.1.refs_11_), channel_id=1, source_target_pairs={{0,2},{8,14},{2,4},{10,8},{4,6},{12,10},{6,0},{14,12},{1,3},{9,15}... | collective-permute-start | bytes 2654216 | tf_op jit(solution)/shard_map/late/ppermute | solution.py:378
  115.3 0.9 copy-start.1
  116.2 4.2 %collective-permute-start.13 = (bf16[384,1152]{1,0:T(8,128)(2,1)}, bf16[384,1152]{1,0:T(8,128)(2,1)S(1)}, u32[]{:S(2)}, u32[]{:S(2)}) collective-permute-start(bf16[384,1152]{1,0:T(8,128)(2,1)} %gate.5.refs_1_), channel_id=1, source_target_pairs={{24,16},{32,40},{25,17},{33,41},{26,18},{34,42},{27,19},{35,43},{2... | collective-permute-start | bytes 2654216 | tf_op jit(solution)/shard_map/over_f1/ppermute | solution.py:475
  116.9 3.5 %copy-start.4 = (bf16[384,1152]{1,0:T(8,128)(2,1)}, bf16[384,1152]{1,0:T(8,128)(2,1)S(1)}, u32[]{:S(2)}) copy-start(bf16[384,1152]{1,0:T(8,128)(2,1)S(1)} %collective-permute-done.15.refs_11_) | copy-start | bytes 2654212
  120.4 0.9 copy-start.3
  120.4 1.2 copy-start.6
